TPU v7x, 128 devices: a whole 4x4x4 slice. The times are simulated.
128 devices in a mesh: scene: 2 (over core), row: 8 (over x, y_lo), col: 8 (over z, y_hi).
Axes of the slice: x: 4, y: 4 (y_hi: 2, y_lo: 2; y = y_hi * 2 + y_lo), z: 4, core: 2. Of those that a mesh axis runs over, the one named last changes fastest.
Arguments:
- activations: bfloat16 [384, 256, 768], P(('scene', 'row'), 'col'), parts along dimension 0, may hold values from -6 to 6
- cotangent: bfloat16 [384, 256, 768], P(('scene', 'row'), 'col'), parts along dimension 0, may hold values from -6 to 6
- qkv_weight: bfloat16 [768, 2304], replicated, may hold values from -1 to 1
- out_weight: bfloat16 [768, 768], replicated, may hold values from -0.21875 to 0.21875
Outputs:
- input_grad: bfloat16 [384, 256, 768], P(('scene', 'row'), 'col'), parts along dimension 0
- qkv_weight_grad: float32 [1536, 2304], P(('scene', 'row', 'col')), parts along dimension 0
- out_weight_grad: float32 [1536, 768], P(('scene', 'row', 'col')), parts along dimension 0
There are 2 independent parts, one for each index of `scene`. A program takes and returns all parts, laid end to end along the dimension named above; an argument that names none is the same for every part. Nothing has to cross between parts.
All inputs are finite; a program needn't handle non-finite values.
Results may differ from a plain program's by a relative error of at most 0.0096.
Values may be sent and summed in bfloat16 or wider, within the bound.
No kernel may reach another device: no remote copies, remote signals or barrier semaphores. Data moves between devices by JAX's collectives and lax.ppermute only.
A program may use at most 128 MiB of HBM per device.

v0:
```python
import jax
import jax.numpy as jnp
from jax import lax
from jax.sharding import PartitionSpec as P

HEADS = 24


EPSILON = 1e-05


def layer_normalize(tokens):
    value_rows = tokens.astype(jnp.float32)
    centred = value_rows - jnp.mean(value_rows, axis=-1, keepdims=True)
    inverse_deviation = lax.rsqrt(jnp.mean(centred * centred, axis=-1, keepdims=True) + EPSILON)
    return (centred * inverse_deviation, inverse_deviation)


def forward_pass(activation_windows, qkv_weight):
    element_count, sequence_length, feature_width = activation_windows.shape
    head_dim = feature_width // HEADS
    scaling = head_dim ** (-0.5)
    standardized_input, inverse_deviation = layer_normalize(activation_windows)
    normalized_input = standardized_input.astype(jnp.bfloat16).reshape(
        element_count * sequence_length, feature_width
    )
    projected = jnp.dot(normalized_input, qkv_weight, preferred_element_type=jnp.float32).astype(
        jnp.bfloat16
    )
    projected = projected.reshape(element_count, sequence_length, 3, HEADS, head_dim)
    query_rows, key_rows, value_rows = (projected[:, :, 0], projected[:, :, 1], projected[:, :, 2])
    scores = (
        jnp.einsum("nqhd,nkhd->nhqk", query_rows, key_rows, preferred_element_type=jnp.float32)
        * scaling
    )
    attention_weights = jax.nn.softmax(scores, axis=-1)
    weights_reduced = attention_weights.astype(jnp.bfloat16)
    attention_output = jnp.einsum(
        "nhqk,nkhd->nqhd", weights_reduced, value_rows, preferred_element_type=jnp.float32
    )
    attention_output = attention_output.astype(jnp.bfloat16).reshape(
        element_count * sequence_length, feature_width
    )
    return (
        standardized_input,
        inverse_deviation,
        normalized_input,
        query_rows,
        key_rows,
        value_rows,
        attention_weights,
        weights_reduced,
        attention_output,
    )


def backward_pass(saved_residuals, cot_groups, qkv_weight, out_weight):
    (
        standardized_input,
        inverse_deviation,
        normalized_input,
        query_rows,
        key_rows,
        value_rows,
        attention_weights,
        weights_reduced,
        attention_output,
    ) = saved_residuals
    element_count, sequence_length, feature_width = cot_groups.shape
    head_dim = feature_width // HEADS
    scaling = head_dim ** (-0.5)
    cot_rows = cot_groups.reshape(element_count * sequence_length, feature_width)
    out_grad = lax.dot_general(
        cot_rows, out_weight, (((1,), (1,)), ((), ())), preferred_element_type=jnp.float32
    )
    out_grad = out_grad.astype(jnp.bfloat16).reshape(
        element_count, sequence_length, HEADS, head_dim
    )
    prob_grad = jnp.einsum(
        "nqhd,nkhd->nhqk", out_grad, value_rows, preferred_element_type=jnp.float32
    )
    value_grad = jnp.einsum(
        "nhqk,nqhd->nkhd", weights_reduced, out_grad, preferred_element_type=jnp.float32
    )
    score_grad = attention_weights * (
        prob_grad - jnp.sum(attention_weights * prob_grad, axis=-1, keepdims=True)
    )
    score_low = score_grad.astype(jnp.bfloat16)
    query_grad = (
        jnp.einsum("nhqk,nkhd->nqhd", score_low, key_rows, preferred_element_type=jnp.float32)
        * scaling
    )
    key_grad = (
        jnp.einsum("nhqk,nqhd->nkhd", score_low, query_rows, preferred_element_type=jnp.float32)
        * scaling
    )
    qkv_grad = jnp.stack([query_grad, key_grad, value_grad], axis=2).astype(jnp.bfloat16)
    qkv_grad = qkv_grad.reshape(element_count * sequence_length, 3 * feature_width)
    normalized_gradient = lax.dot_general(
        qkv_grad, qkv_weight, (((1,), (1,)), ((), ())), preferred_element_type=jnp.float32
    )
    normalized_gradient = normalized_gradient.reshape(element_count, sequence_length, feature_width)
    centered_gradient = normalized_gradient - jnp.mean(normalized_gradient, axis=-1, keepdims=True)
    centered_gradient = centered_gradient - standardized_input * jnp.mean(
        normalized_gradient * standardized_input, axis=-1, keepdims=True
    )
    input_grad = (cot_groups.astype(jnp.float32) + inverse_deviation * centered_gradient).astype(
        jnp.bfloat16
    )
    return (input_grad, qkv_grad, cot_rows)


def local(activations, cotangent, qkv_weight, out_weight):
    grid_rows = lax.axis_size("row")
    grid_cols = lax.axis_size("col")
    rows_dev, cols_dev, feature_width = activations.shape
    part_rows = rows_dev // grid_rows
    part_cols = cols_dev // grid_cols

    def arrange(field):
        return field.reshape(grid_rows, part_rows, grid_cols, part_cols, feature_width)

    def regroup(block):
        return block.transpose(1, 3, 0, 2, 4).reshape(
            part_rows * part_cols, grid_rows * grid_cols, feature_width
        )

    act_grid, cot_grid = (
        lax.all_to_all(
            lax.all_to_all(arrange(activations), "row", split_axis=0, concat_axis=0, tiled=True),
            "col",
            split_axis=2,
            concat_axis=2,
            tiled=True,
        ),
        lax.all_to_all(
            lax.all_to_all(arrange(cotangent), "row", split_axis=0, concat_axis=0, tiled=True),
            "col",
            split_axis=2,
            concat_axis=2,
            tiled=True,
        ),
    )
    saved_residuals = forward_pass(regroup(act_grid), qkv_weight)
    cot_groups = regroup(cot_grid)
    grad_groups, qkv_grad, cot_rows = backward_pass(
        saved_residuals, cot_groups, qkv_weight, out_weight
    )
    normalized_input = saved_residuals[2]
    attention_output = saved_residuals[8]
    grad_block = grad_groups.reshape(
        part_rows, part_cols, grid_rows, grid_cols, feature_width
    ).transpose(2, 0, 3, 1, 4)
    home_grad = lax.all_to_all(
        lax.all_to_all(grad_block, "row", split_axis=0, concat_axis=0, tiled=True),
        "col",
        split_axis=2,
        concat_axis=2,
        tiled=True,
    )
    input_grad = home_grad.reshape(rows_dev, cols_dev, feature_width)
    first_term = lax.dot_general(
        normalized_input, qkv_grad, (((0,), (0,)), ((), ())), preferred_element_type=jnp.float32
    )
    second_term = lax.dot_general(
        attention_output, cot_rows, (((0,), (0,)), ((), ())), preferred_element_type=jnp.float32
    )
    summed = lax.psum_scatter(
        jnp.concatenate([first_term, second_term], axis=1),
        ("row", "col"),
        scatter_dimension=0,
        tiled=True,
    )
    qkv_weight_grad = summed[:, : 3 * feature_width]
    out_weight_grad = summed[:, 3 * feature_width :]
    return (input_grad, qkv_weight_grad, out_weight_grad)


def solution(mesh):
    return jax.shard_map(
        local,
        mesh=mesh,
        in_specs=(P(("scene", "row"), "col", None), P(("scene", "row"), "col", None), P(), P()),
        out_specs=(
            P(("scene", "row"), "col", None),
            P(("scene", "row", "col"), None),
            P(("scene", "row", "col"), None),
        ),
        check_vma=False,
    )
```

profile of v0, /device:TPU:0, one launch (start us, length us, event | category | flops | bytes accessed | tf_op | source)
XLA Modules:
  0.0 482.7 jit_solution(12199024785059790629)
XLA Ops:
  13.1 5.4 %all-to-all-start.2 = ((bf16[8,3,8,4,768]{4,2,3,1,0:T(8,128)(2,1)}), bf16[8,3,8,4,768]{4,2,3,1,0:T(8,128)(2,1)}, u32[]{:S(2)}, u32[]{:S(2)}) async-start(bf16[8,3,8,4,768]{4,2,3,1,0:T(8,128)(2,1)} %copy.66), calls=%async_computation.2 | async-start | bytes 2359296 | tf_op jit(solution)/shard_map/all_to_all | solution.py:130
  24.2 12.3 %all-to-all-done.2 = bf16[8,3,8,4,768]{4,2,3,1,0:T(8,128)(2,1)} async-done(((bf16[8,3,8,4,768]{4,2,3,1,0:T(8,128)(2,1)}), bf16[8,3,8,4,768]{4,2,3,1,0:T(8,128)(2,1)}, u32[]{:S(2)}, u32[]{:S(2)}) %all-to-all-start.2) | async-done | bytes 1179680 | tf_op jit(solution)/shard_map/all_to_all | solution.py:130
  43.7 13.6 %all-to-all-done = bf16[8,3,8,4,768]{4,2,3,1,0:T(8,128)(2,1)} async-done(((bf16[8,3,8,4,768]{4,2,3,1,0:T(8,128)(2,1)}), bf16[8,3,8,4,768]{4,2,3,1,0:T(8,128)(2,1)}, u32[]{:S(2)}, u32[]{:S(2)}) %all-to-all-start) | async-done | bytes 1179680 | tf_op jit(solution)/shard_map/all_to_all | solution.py:137
  57.3 7.7 %all-to-all-start.3 = ((bf16[8,3,8,4,768]{4,0,3,1,2:T(8,128)(2,1)}), bf16[8,3,8,4,768]{4,0,3,1,2:T(8,128)(2,1)}, u32[]{:S(2)}, u32[]{:S(2)}) async-start(bf16[8,3,8,4,768]{4,0,3,1,2:T(8,128)(2,1)} %copy.67), calls=%async_computation.3 | async-start | bytes 2359296 | tf_op jit(solution)/shard_map/all_to_all | solution.py:129
  67.9 14.5 %all-to-all-done.3 = bf16[8,3,8,4,768]{4,0,3,1,2:T(8,128)(2,1)} async-done(((bf16[8,3,8,4,768]{4,0,3,1,2:T(8,128)(2,1)}), bf16[8,3,8,4,768]{4,0,3,1,2:T(8,128)(2,1)}, u32[]{:S(2)}, u32[]{:S(2)}) %all-to-all-start.3) | async-done | bytes 1179680 | tf_op jit(solution)/shard_map/all_to_all | solution.py:129
  96.3 4.8 convolution_convert_fusion
  101.1 16.4 %reshape.126 = bf16[12,64,3,24,32]{4,3,2,1,0:T(8,128)(2,1)} reshape(bf16[768,2304]{1,0:T(8,128)(2,1)} %convolution_convert_fusion) | data formatting | bytes 7077888 | tf_op jit(solution)/shard_map/reshape | solution.py:30
  117.5 11.2 %fusion.37 = (bf16[12,64,1,24,32]{4,3,2,1,0:T(8,128)(2,1)}, bf16[12,64,1,24,32]{4,3,2,1,0:T(8,128)(2,1)}, bf16[12,64,1,24,32]{4,3,2,1,0:T(8,128)(2,1)}) fusion(bf16[12,64,3,24,32]{4,3,2,1,0:T(8,128)(2,1)} %reshape.126), kind=kLoop, calls=%fused_computation.52 | loop fusion | bytes 7077888 | tf_op jit(solution)/shard_map/slice | solution.py:31
  128.7 6.3 %copy.98 = bf16[12,64,1,24,32]{1,4,3,0,2:T(8,128)(2,1)} copy(bf16[12,64,1,24,32]{4,3,2,1,0:T(8,128)(2,1)} %get-tuple-element.7) | data formatting | bytes 2359296
  135.0 6.3 %copy.99 = bf16[12,64,1,24,32]{1,4,3,0,2:T(8,128)(2,1)} copy(bf16[12,64,1,24,32]{4,3,2,1,0:T(8,128)(2,1)} %get-tuple-element.6) | data formatting | bytes 2359296
  141.3 6.4 %copy.100 = bf16[12,64,1,24,32]{1,4,3,0,2:T(8,128)(2,1)} copy(bf16[12,64,1,24,32]{4,3,2,1,0:T(8,128)(2,1)} %get-tuple-element.5) | data formatting | bytes 2359296
  151.5 5.7 %fusion.38 = (f32[12,24,64]{2,1,0:T(8,128)}, f32[12,24,64,64]{2,3,1,0:T(8,128)}) fusion(f32[12,24,64,64]{2,3,1,0:T(8,128)S(1)} %fusion.16), kind=kOutput, calls=%fused_computation.53 | output fusion | flops 4718655 | bytes 9510912 | tf_op jit(solution)/shard_map/sub | solution.py:36
  162.4 6.4 %reshape.127 = bf16[12,64,24,32]{3,2,1,0:T(8,128)(2,1)} reshape(bf16[768,768]{1,0:T(8,128)(2,1)} %convolution_convert_fusion.1) | data formatting | bytes 2359296 | tf_op jit(solution)/shard_map/reshape | solution.py:76
  168.8 6.5 %copy.74 = bf16[12,64,24,32]{1,3,2,0:T(8,128)(2,1)} copy(bf16[12,64,24,32]{3,2,1,0:T(8,128)(2,1)} %reshape.127) | data formatting | bytes 2359296 | tf_op jit(solution)/shard_map/reshape | solution.py:76
  175.3 11.8 %multiply_reduce_fusion = (f32[12,24,64]{2,1,0:T(8,128)}, f32[12,24,64,64]{2,3,1,0:T(8,128)}) fusion(f32[12,24,64,64]{2,3,1,0:T(8,128)} %get-tuple-element.9, f32[12,24,64]{2,1,0:T(8,128)} %get-tuple-element.8, bf16[12,64,24,32]{1,3,2,0:T(8,128)(2,1)} %copy.74, bf16[12,64,1,24,32]{1,4,3,0,2:T(8,128)(2,1)} %copy.100), kind=kOutput, calls=%fused_computation.4 | convolution fusion | flops 79017984 | bytes 11943936 | tf_op jit(solution)/shard_map/nqhd,nkhd->nhqk/dot_general | solution.py:79
  187.1 11.6 %multiply_convert_fusion = bf16[12,24,64,64]{2,3,1,0:T(8,128)(2,1)} fusion(f32[12,24,64,64]{2,3,1,0:T(8,128)} %get-tuple-element.11, f32[12,24,64]{2,1,0:T(8,128)} %get-tuple-element.10, f32[12,24,64,64]{2,3,1,0:T(8,128)} %get-tuple-element.9, f32[12,24,64]{2,1,0:T(8,128)} %get-tuple-element.8), kind=kLoop, calls=%fused_computation.3 | loop fusion | flops 4718592 | bytes 11943936 | tf_op jit(solution)/shard_map/convert_element_type | solution.py:88
  198.7 4.5 multiply_bitcast_fusion.1
  206.6 8.5 %fusion.24 = bf16[12,64,1,24,32]{1,4,3,0,2:T(8,128)(2,1)} fusion(bf16[12,64,24,32]{1,3,2,0:T(8,128)(2,1)} %copy.74, f32[12,24,64,64]{2,3,1,0:T(8,128)} %get-tuple-element.9, f32[12,24,64]{2,1,0:T(8,128)S(1)} %copy-done.9), kind=kOutput, calls=%fused_computation.41 | convolution fusion | flops 77856768 | bytes 7151616 | tf_op jit(solution)/shard_map/nhqk,nqhd->nkhd/dot_general | solution.py:82
  215.1 4.6 convert_bitcast_fusion
  223.9 15.2 %copy.84 = bf16[12,64,3,24,32]{1,0,4,3,2:T(8,128)(2,1)} copy(bf16[12,64,3,24,32]{1,4,3,0,2:T(8,128)(2,1)} %maximum_convert_fusion) | data formatting | bytes 7077888 | tf_op jit(solution)/shard_map/convert_element_type | solution.py:97
  239.1 12.0 %convert_element_type.93 = bf16[768,2304]{0,1:T(8,128)(2,1)} reshape(bf16[12,64,3,24,32]{1,0,4,3,2:T(8,128)(2,1)} %copy.84) | data formatting | bytes 7077888 | tf_op jit(solution)/shard_map/convert_element_type | solution.py:97
  251.0 4.9 %copy.86 = bf16[12,64,24,32]{1,0,3,2:T(8,128)(2,1)} copy(bf16[12,64,24,32]{1,3,2,0:T(8,128)(2,1)} %convert_bitcast_fusion) | data formatting | bytes 2359296 | tf_op jit(solution)/shard_map/convert_element_type | solution.py:41
  256.0 5.0 %reshape.120 = bf16[768,768]{0,1:T(8,128)(2,1)} reshape(bf16[12,64,24,32]{1,0,3,2:T(8,128)(2,1)} %copy.86) | data formatting | bytes 2359296 | tf_op jit(solution)/shard_map/reshape | solution.py:41
  261.0 4.3 fusion.40
  267.9 5.0 %fusion.39 = f32[768,2304]{1,0:T(8,128)} fusion(bf16[768,768]{1,0:T(8,128)(2,1)S(1)} %bitcast.106, bf16[768,2304]{0,1:T(8,128)(2,1)S(1)} %copy-done.5), kind=kOutput, calls=%fused_computation.54 | convolution fusion | flops 2717908992 | bytes 11796480 | tf_op jit(solution)/shard_map/dot_general | solution.py:162
  272.9 8.8 %pad_maximum_fusion = f32[768,3072]{1,0:T(8,128)} fusion(f32[768,768]{1,0:T(8,128)} %fusion.40, f32[768,2304]{1,0:T(8,128)} %fusion.39), kind=kLoop, calls=%fused_computation.2 | loop fusion | flops 2359296 | bytes 18874368 | tf_op jit(solution)/shard_map/concatenate | solution.py:169
  281.7 7.8 %copy.79 = bf16[12,64,3,24,32]{1,4,3,2,0:T(8,128)(2,1)} copy(bf16[12,64,3,24,32]{1,4,3,0,2:T(8,128)(2,1)} %maximum_convert_fusion) | data formatting | bytes 7077888 | tf_op jit(solution)/shard_map/convert_element_type | solution.py:97
  293.3 8.4 %fusion.36 = (f32[12,64]{1,0:T(8,128)S(1)}, f32[12,64]{1,0:T(8,128)S(1)}, f32[12,64,768]{2,1,0:T(8,128)S(1)}) fusion(f32[12,64]{1,0:T(8,128)S(1)} %rsqrt.17, f32[12,64,768]{2,1,0:T(8,128)S(1)} %bitcast.98, f32[12,64]{1,0:T(8,128)S(1)} %div.30, bf16[12,64,2304]{1,2,0:T(8,128)(2,1)} %bitcast.100, bf16[768,2304]{1,0:T(8,128)(2,1)S(1)} %copy-done), kind=kOutput, calls=%fused_computation.51 | convolution fusion | flops 2720856576 | bytes 11808768 | tf_op jit(solution)/shard_map/dot_general | solution.py:99
  302.8 31.3 %all_to_all.30 = bf16[8,3,8,4,768]{4,2,3,1,0:T(8,128)(2,1)S(1)} all-to-all(bf16[8,3,8,4,768]{4,2,3,1,0:T(8,128)(2,1)S(1)} %bitcast.105), channel_id=1, replica_groups=mesh['scene'=2,'row'=8,'col'=8] {'row'}, dimensions={0} | all-to-all | bytes 2359296 | tf_op jit(solution)/shard_map/all_to_all | solution.py:155
  335.7 5.1 %all-to-all-start.5 = ((bf16[8,3,8,4,768]{4,0,3,1,2:T(8,128)(2,1)}), bf16[8,3,8,4,768]{4,0,3,1,2:T(8,128)(2,1)}, u32[]{:S(2)}, u32[]{:S(2)}) async-start(bf16[8,3,8,4,768]{4,0,3,1,2:T(8,128)(2,1)} %copy.82), calls=%async_computation.5 | async-start | bytes 2359296 | tf_op jit(solution)/shard_map/all_to_all | solution.py:154
  342.1 22.1 %all-to-all-done.5 = bf16[8,3,8,4,768]{4,0,3,1,2:T(8,128)(2,1)} async-done(((bf16[8,3,8,4,768]{4,0,3,1,2:T(8,128)(2,1)}), bf16[8,3,8,4,768]{4,0,3,1,2:T(8,128)(2,1)}, u32[]{:S(2)}, u32[]{:S(2)}) %all-to-all-start.5) | async-done | bytes 1179680 | tf_op jit(solution)/shard_map/all_to_all | solution.py:154
  370.3 101.9 %all-reduce.3.cloned.1.call-done = f32[768,3072]{1,0:T(8,128)} async-done(((f32[768,3072]{1,0:T(8,128)}), f32[768,3072]{1,0:T(8,128)}) %all-reduce.3.cloned.1.call-update) | async-done | bytes 9437200
  (67 shorter events, 71.1 us)
Async XLA Ops:
  7.2 89.1 %copy-start = (bf16[768,2304]{1,0:T(8,128)(2,1)S(1)}, bf16[768,2304]{1,0:T(8,128)(2,1)}, u32[]{:S(2)}) copy-start(bf16[768,2304]{1,0:T(8,128)(2,1)} %param.6) | copy-start | bytes 10616836
  13.1 23.4 %all-to-all-start.2 = ((bf16[8,3,8,4,768]{4,2,3,1,0:T(8,128)(2,1)}), bf16[8,3,8,4,768]{4,2,3,1,0:T(8,128)(2,1)}, u32[]{:S(2)}, u32[]{:S(2)}) async-start(bf16[8,3,8,4,768]{4,2,3,1,0:T(8,128)(2,1)} %copy.66), calls=%async_computation.2 | async-start | bytes 2359296 | tf_op jit(solution)/shard_map/all_to_all | solution.py:130
  36.5 20.8 %all-to-all-start = ((bf16[8,3,8,4,768]{4,2,3,1,0:T(8,128)(2,1)}), bf16[8,3,8,4,768]{4,2,3,1,0:T(8,128)(2,1)}, u32[]{:S(2)}, u32[]{:S(2)}) async-start(bf16[8,3,8,4,768]{4,2,3,1,0:T(8,128)(2,1)} %copy.63), calls=%async_computation | async-start | bytes 2359296 | tf_op jit(solution)/shard_map/all_to_all | solution.py:137
  57.3 25.1 %all-to-all-start.3 = ((bf16[8,3,8,4,768]{4,0,3,1,2:T(8,128)(2,1)}), bf16[8,3,8,4,768]{4,0,3,1,2:T(8,128)(2,1)}, u32[]{:S(2)}, u32[]{:S(2)}) async-start(bf16[8,3,8,4,768]{4,0,3,1,2:T(8,128)(2,1)} %copy.67), calls=%async_computation.3 | async-start | bytes 2359296 | tf_op jit(solution)/shard_map/all_to_all | solution.py:129
  82.4 74.8 %all-to-all-start.1 = ((bf16[8,3,8,4,768]{4,0,3,1,2:T(8,128)(2,1)}), bf16[8,3,8,4,768]{4,0,3,1,2:T(8,128)(2,1)}, u32[]{:S(2)}, u32[]{:S(2)}) async-start(bf16[8,3,8,4,768]{4,0,3,1,2:T(8,128)(2,1)} %copy.64), calls=%async_computation.1 | async-start | bytes 2359296 | tf_op jit(solution)/shard_map/all_to_all | solution.py:136
  86.6 385.5 %all-reduce.3.cloned.1.call-start = ((), (), s32[]{:S(2)}) async-start(), calls=%async_computation.6 | async-start | bytes 18874368
  157.2 3.0 copy-start.10
  159.2 1.0 copy-start.3
  198.7 4.6 copy-start.1
  198.7 5.2 %copy-start.2 = (bf16[12,64,1,24,32]{1,4,3,0,2:T(8,128)(2,1)S(1)}, bf16[12,64,1,24,32]{1,4,3,0,2:T(8,128)(2,1)}, u32[]{:S(2)}) copy-start(bf16[12,64,1,24,32]{1,4,3,0,2:T(8,128)(2,1)} %copy.99) | copy-start | bytes 3538948
  203.9 2.7 copy-start.9
  203.9 11.2 %slice-start = ((s8[9437184]{0:T(1024)(128)(4,1)}), s8[4194304]{0:T(1024)(128)(4,1)S(1)}, s32[]{:S(2)}) async-start(s8[9437184]{0:T(1024)(128)(4,1)} %bitcast.96), calls=%async_computation.7 | async-start | bytes 8388608
  206.6 8.5 %slice-start.1 = ((s8[9437184]{0:T(1024)(128)(4,1)}), s8[4194304]{0:T(1024)(128)(4,1)S(1)}, s32[]{:S(2)}) async-start(s8[9437184]{0:T(1024)(128)(4,1)} %bitcast.96), calls=%async_computation.8 | async-start | bytes 8388608
  206.6 8.5 %slice-start.2 = ((s8[9437184]{0:T(1024)(128)(4,1)}), s8[1048576]{0:T(1024)(128)(4,1)S(1)}, s32[]{:S(2)}) async-start(s8[9437184]{0:T(1024)(128)(4,1)} %bitcast.96), calls=%async_computation.9 | async-start | bytes 2097152
  215.1 4.6 copy-start.6
  260.9 4.3 copy-start.7
  260.9 4.3 copy-start.8
  261.0 6.9 %copy-start.5 = (bf16[768,2304]{0,1:T(8,128)(2,1)S(1)}, bf16[768,2304]{0,1:T(8,128)(2,1)}, u32[]{:S(2)}) copy-start(bf16[768,2304]{0,1:T(8,128)(2,1)} %convert_element_type.93) | copy-start | bytes 10616836
  293.3 8.4 %copy-start.4 = (bf16[8,3,8,4,768]{4,2,0,3,1:T(8,128)(2,1)S(1)}, bf16[8,3,8,4,768]{4,2,0,3,1:T(8,128)(2,1)}, u32[]{:S(2)}) copy-start(bf16[8,3,8,4,768]{4,2,0,3,1:T(8,128)(2,1)} %copy-done.3) | copy-start | bytes 3538948
  334.1 6.7 %copy-start.11 = (u32[128]{0:T(128)S(1)}, u32[128]{0:T(128)}, u32[]{:S(2)}) copy-start(u32[128]{0:T(128)} %constant.20) | copy-start | bytes 1540
  335.7 28.5 %all-to-all-start.5 = ((bf16[8,3,8,4,768]{4,0,3,1,2:T(8,128)(2,1)}), bf16[8,3,8,4,768]{4,0,3,1,2:T(8,128)(2,1)}, u32[]{:S(2)}, u32[]{:S(2)}) async-start(bf16[8,3,8,4,768]{4,0,3,1,2:T(8,128)(2,1)} %copy.82), calls=%async_computation.5 | async-start | bytes 2359296 | tf_op jit(solution)/shard_map/all_to_all | solution.py:154
Sparse Core Ops, SparseCore 0:
  281.8 190.2 all-reduce.2
where the time goes:
time: 490 us; the launch traced here: 483 us
  waiting for transfers between devices  164 us (33%)
  local copies, waits for them, and re-layouts  141 us (29%)
  matrix products  60.5 us (12%)
  other arithmetic  43.6 us (9%)
  blocking collectives  31.3 us (6%)
  starting transfers between devices  26.7 us (5%)
  between operations  15.4 us (3%)
    unnamed x2, waiting for transfers between devices  102 us
    convert_element_type x3, local copies, waits for them, and re-layouts, backward_pass(): jnp.stack([query_grad, key_grad, value_grad], axis=2).astype(jnp.bfloat16)  35 us
    all_to_all x1, blocking collectives, local(): lax.all_to_all(grad_block, 'row', split_axis=0, concat_axis=0, tiled=True)  31.3 us
    all_to_all x1, waiting for transfers between devices, local(): lax.all_to_all(lax.all_to_all(grad_block, 'row', split_axis=0, concat_axi...  22.1 us
    unnamed x34, local copies, waits for them, and re-layouts  21.3 us
    reshape x1, local copies, waits for them, and re-layouts, forward_pass(): projected.reshape(element_count, sequence_length, 3, HEADS, head_dim)  16.4 us
    all_to_all x1, waiting for transfers between devices, local(): lax.all_to_all(lax.all_to_all(arrange(activations), 'row', split_axis=0,...  14.5 us
    all_to_all x1, waiting for transfers between devices, local(): lax.all_to_all(arrange(cotangent), 'row', split_axis=0, concat_axis=0, ti...  13.6 us
  transfers between devices with their start and end apart: 6, of which 5 were waited for; matrix products, arithmetic and copies ran while one was open for 23% of the time, Pallas kernels for 0%

commit v1 on v0

v1 whole, which is shorter than its diff:
```python
import functools

import jax
import jax.numpy as jnp
from jax import lax
from jax.experimental import pallas as pl
from jax.experimental.pallas import tpu as pltpu
from jax.sharding import PartitionSpec as P

HEADS = 24
EPSILON = 1e-05
BF16 = jnp.bfloat16
F32 = jnp.float32
MIB = 1 << 20


def dot(a, b, dims):
    return lax.dot_general(a, b, ((dims[0], dims[1]), ((), ())), preferred_element_type=F32)


def nn(a, b):
    return dot(a, b, ((1,), (0,)))


def nt(a, b):
    return dot(a, b, ((1,), (1,)))


def tn(a, b):
    return dot(a, b, ((0,), (0,)))


def one_hot(shape, column_of_row):
    rows = lax.broadcasted_iota(jnp.int32, shape, 0)
    columns = lax.broadcasted_iota(jnp.int32, shape, 1)
    return jnp.where(columns == column_of_row(rows), 1.0, 0.0).astype(BF16)


def pack_kernel(act_main, act_tail, cot_main, cot_tail, out):
    rows, width = act_main.shape
    half = width // 2
    upper = one_hot((rows, rows // 2), lambda i: jnp.where(i % 8 < 4, (i // 8) * 4 + i % 4, -1))
    lower = one_hot((rows, rows // 2), lambda i: jnp.where(i % 8 < 4, -1, (i // 8) * 4 + i % 4))
    at = 0
    for main, tail in ((act_main, act_tail), (cot_main, cot_tail)):
        out[:, at : at + width] = main[...]
        packed = nn(upper, tail[:, :half]) + nn(lower, tail[:, half:])
        out[:, at + width : at + width + half] = packed.astype(BF16)
        at += width + half


def pack_tokens(act, cot, peers):
    tokens, width = act.shape
    steps = 4
    rows = peers * 8 // steps
    main = pl.BlockSpec((rows, width), lambda i: (i, 0))
    tail = pl.BlockSpec((rows // 2, width), lambda i: (2 * steps + i, 0))
    return pl.pallas_call(
        pack_kernel,
        grid=(steps,),
        in_specs=[main, tail, main, tail],
        out_specs=pl.BlockSpec((rows, 3 * width), lambda i: (i, 0)),
        out_shape=jax.ShapeDtypeStruct((peers * 8, 3 * width), BF16),
        compiler_params=pltpu.CompilerParams(vmem_limit_bytes=32 * MIB),
        name="pack_tokens",
    )(act, act, cot, cot)


def main_kernel(
    got, qkv_w, out_w, out, xs, ns, cs, qkv, og, dqkv, att, ngs, mean_s, inv_s, nt1, nt2, at1, at2, order
):
    width = out_w.shape[0]
    half = width // 2
    tokens = xs.shape[0]
    seq = 64
    main = got.shape[0]
    rest = tokens - main
    packed = width + half
    head_dim = width // HEADS
    scaling = head_dim**-0.5

    order[...] = one_hot((main, main), lambda k: (k % seq) * 8 + k // seq)
    for first, to in ((0, xs), (packed, cs)):
        for c in range(0, width, half):
            to[:main, c : c + half] = nn(order[...], got[:, first + c : first + c + half]).astype(BF16)
        tail = nn(order[...], got[:, first + width : first + packed]).astype(BF16)
        to[main:, :half] = tail[:rest]
        to[main:, half:] = tail[rest:]

    @pl.loop(0, tokens // seq)
    def _(g):
        rows = pl.ds(pl.multiple_of(g * seq, seq), seq)
        x = xs[rows, :].astype(F32)
        mean = jnp.mean(x, axis=-1, keepdims=True)
        centred = x - mean
        inv = lax.rsqrt(jnp.mean(centred * centred, axis=-1, keepdims=True) + EPSILON)
        ns[rows, :] = (centred * inv).astype(BF16)
        mean_s[rows, :] = jnp.broadcast_to(mean, (seq, 128))
        inv_s[rows, :] = jnp.broadcast_to(inv, (seq, 128))

    @pl.loop(0, 3 * width // 256)
    def _(j):
        cols = pl.ds(pl.multiple_of(j * 256, 256), 256)
        qkv[:, cols] = nn(ns[...], qkv_w[:, cols]).astype(BF16)

    @pl.loop(0, width // 256)
    def _(j):
        cols = pl.ds(pl.multiple_of(j * 256, 256), 256)
        og[:, cols] = nt(cs[...], out_w[cols, :]).astype(BF16)

    lanes = 128
    heads = lanes // head_dim
    wide = heads * seq
    own = lax.broadcasted_iota(jnp.int32, (wide, lanes), 0) // seq
    keep = jnp.where(lax.broadcasted_iota(jnp.int32, (wide, lanes), 1) // head_dim == own, 1.0, 0.0).astype(BF16)
    lane_head = lax.broadcasted_iota(jnp.int32, (seq, lanes), 1) // head_dim

    def spread(x):
        return jnp.concatenate([x] * heads, axis=0) * keep

    def fold(x):
        total = x[:seq]
        for h in range(1, heads):
            total = jnp.where(lane_head == h, x[h * seq : (h + 1) * seq], total)
        return total

    @pl.loop(0, tokens // seq)
    def _(g):
        rows = pl.ds(pl.multiple_of(g * seq, seq), seq)
        for c in range(0, width, lanes):
            q = qkv[rows, c : c + lanes]
            k = qkv[rows, width + c : width + c + lanes]
            v = qkv[rows, 2 * width + c : 2 * width + c + lanes]
            q_wide = spread(q)
            g_wide = spread(og[rows, c : c + lanes])
            scores = nt(k, q_wide)
            top = jnp.max(scores, axis=0, keepdims=True)
            e = jnp.exp((scores - top) * scaling)
            probs = e * (1.0 / jnp.sum(e, axis=0, keepdims=True))
            probs_low = probs.astype(BF16)
            prob_grad = nt(v, g_wide)
            delta = jnp.sum(probs * prob_grad, axis=0, keepdims=True)
            score_low = (probs * (prob_grad - delta)).astype(BF16)
            att[rows, c : c + lanes] = fold(tn(probs_low, v)).astype(BF16)
            dqkv[rows, c : c + lanes] = (fold(tn(score_low, k)) * scaling).astype(BF16)
            dqkv[rows, width + c : width + c + lanes] = (nn(score_low, q_wide) * scaling).astype(BF16)
            dqkv[rows, 2 * width + c : 2 * width + c + lanes] = nn(probs_low, g_wide).astype(BF16)

    @pl.loop(0, width // 256)
    def _(j):
        cols = pl.ds(pl.multiple_of(j * 256, 256), 256)
        ngs[:, cols] = nt(dqkv[...], qkv_w[cols, :])

    @pl.loop(0, tokens // seq)
    def _(g):
        rows = pl.ds(pl.multiple_of(g * seq, seq), seq)
        inv = inv_s[rows, :][:, :1]
        xhat = (xs[rows, :].astype(F32) - mean_s[rows, :][:, :1]) * inv
        ng = ngs[rows, :]
        centred = ng - jnp.mean(ng, axis=-1, keepdims=True)
        centred = centred - xhat * jnp.mean(ng * xhat, axis=-1, keepdims=True)
        xs[rows, :] = (cs[rows, :].astype(F32) + inv * centred).astype(BF16)

    back = one_hot((main, main), lambda i: (i % 8) * seq + i // 8)
    for c in range(0, width, half):
        out[:, c : c + half] = nn(back, xs[:main, c : c + half]).astype(BF16)
    tail = nn(back[:, :rest], xs[main:, :half]) + nn(back[:, rest:], xs[main:, half:])
    out[:, width:packed] = tail.astype(BF16)

    eight = one_hot((main, width), lambda i: (i // 8) * 12 + i % 8)
    four = one_hot((main, width), lambda i: (i // 8) * 12 + 8 + i % 4)
    nt1[...] = nt(eight, ns[...]).astype(BF16)
    nt2[...] = nt(four, ns[...]).astype(BF16)
    at1[...] = nt(eight, att[...]).astype(BF16)
    at2[...] = nt(four, att[...]).astype(BF16)

    @pl.loop(0, 3 * width // 256)
    def _(j):
        cols = pl.ds(pl.multiple_of(j * 256, 256), 256)
        to = pl.ds(pl.multiple_of(packed + j * 256, 128), 256)
        out[:, to] = nn(nt1[...], dqkv[:, cols]).astype(BF16)

    @pl.loop(0, width // 256)
    def _(j):
        cols = pl.ds(pl.multiple_of(j * 256, 256), 256)
        to = pl.ds(pl.multiple_of(packed + 3 * width + j * 256, 128), 256)
        out[:, to] = nn(at1[...], cs[:, cols]).astype(BF16)

    first = packed + 4 * width
    is_upper = lax.broadcasted_iota(jnp.int32, (main, 256), 0) % 8 < 4

    @pl.loop(0, width // 256)
    def _(j):
        a = pl.ds(pl.multiple_of(j * 256, 256), 256)
        b = pl.ds(pl.multiple_of(2 * width + j * 256, 256), 256)
        to = pl.ds(pl.multiple_of(first + j * 256, 128), 256)
        pair = jnp.where(is_upper, nn(nt2[...], dqkv[:, a]), nn(nt2[...], dqkv[:, b]))
        out[:, to] = pair.astype(BF16)

    @pl.loop(0, width // 256)
    def _(j):
        a = pl.ds(pl.multiple_of(width + j * 256, 256), 256)
        b = pl.ds(pl.multiple_of(j * 256, 256), 256)
        to = pl.ds(pl.multiple_of(first + width + j * 256, 128), 256)
        pair = jnp.where(is_upper, nn(nt2[...], dqkv[:, a]), nn(at2[...], cs[:, b]))
        out[:, to] = pair.astype(BF16)


def group_backward(got, qkv_weight, out_weight, tokens):
    width = out_weight.shape[0]
    main = got.shape[0]
    vmem = pl.BlockSpec(memory_space=pltpu.VMEM)
    square = (tokens, width)
    scratch = [
        pltpu.VMEM(square, BF16),
        pltpu.VMEM(square, BF16),
        pltpu.VMEM(square, BF16),
        pltpu.VMEM((tokens, 3 * width), BF16),
        pltpu.VMEM(square, BF16),
        pltpu.VMEM((tokens, 3 * width), BF16),
        pltpu.VMEM(square, BF16),
        pltpu.VMEM(square, F32),
        pltpu.VMEM((tokens, 128), F32),
        pltpu.VMEM((tokens, 128), F32),
        pltpu.VMEM((main, tokens), BF16),
        pltpu.VMEM((main, tokens), BF16),
        pltpu.VMEM((main, tokens), BF16),
        pltpu.VMEM((main, tokens), BF16),
        pltpu.VMEM((main, main), BF16),
    ]
    return pl.pallas_call(
        main_kernel,
        in_specs=[vmem] * 3,
        out_specs=vmem,
        out_shape=jax.ShapeDtypeStruct((main, 3 * width // 2 + 6 * width), BF16),
        scratch_shapes=scratch,
        compiler_params=pltpu.CompilerParams(vmem_limit_bytes=56 * MIB),
        name="group_backward",
    )(got, qkv_weight, out_weight)


def finish_kernel(got, grad, qkv_grad, out_grad, total):
    step = pl.program_id(0)
    rows = got.shape[0]
    width = grad.shape[1]
    half = width // 2
    packed = width + half
    main = 8 * grad.shape[0] // 12
    grad[pl.ds(pl.multiple_of(step * rows, 16), rows), :] = got[:, :width]
    pick = one_hot((rows // 2, rows), lambda k: (k // 4) * 8 + k % 4)
    pick_low = one_hot((rows // 2, rows), lambda k: (k // 4) * 8 + 4 + k % 4)
    tail = pl.ds(pl.multiple_of(main + step * (rows // 2), 16), rows // 2)
    grad[tail, :half] = nn(pick, got[:, width:packed]).astype(BF16)
    grad[tail, half:] = nn(pick_low, got[:, width:packed]).astype(BF16)

    @pl.when(step == 0)
    def _():
        total[...] = jnp.zeros_like(total)

    cols = 4 * width + 2 * width
    for c in range(0, cols, width):
        part = got[:, packed + c : packed + c + width].astype(F32).reshape(rows // 8, 8, width)
        total[:, c : c + width] += jnp.sum(part, axis=0)

    @pl.when(step == pl.num_programs(0) - 1)
    def _():
        qkv_grad[:8, :] = total[:, : 3 * width]
        out_grad[:8, :] = total[:, 3 * width : 4 * width]
        qkv_grad[8:12, : 2 * width] = total[:4, 4 * width :]
        qkv_grad[8:12, 2 * width :] = total[4:, 4 * width : 5 * width]
        out_grad[8:12, :] = total[4:, 5 * width :]


def finish(got, tokens, width):
    steps = 4
    rows = got.shape[0] // steps
    whole = lambda shape: pl.BlockSpec(shape, lambda i: (0, 0))
    shapes = ((tokens, width), (12, 3 * width), (12, width))
    return pl.pallas_call(
        finish_kernel,
        grid=(steps,),
        in_specs=[pl.BlockSpec((rows, got.shape[1]), lambda i: (i, 0))],
        out_specs=[whole(s) for s in shapes],
        out_shape=[jax.ShapeDtypeStruct(s, d) for s, d in zip(shapes, (BF16, F32, F32), strict=True)],
        scratch_shapes=[pltpu.VMEM((8, 6 * width), F32)],
        compiler_params=pltpu.CompilerParams(vmem_limit_bytes=32 * MIB),
        name="finish",
    )(got)


def local(activations, cotangent, qkv_weight, out_weight):
    peers = lax.axis_size("row") * lax.axis_size("col")
    rows_dev, cols_dev, width = activations.shape
    tokens = rows_dev * cols_dev
    exchange = functools.partial(
        lax.all_to_all, axis_name=("row", "col"), split_axis=0, concat_axis=0, tiled=True
    )
    sent = pack_tokens(activations.reshape(tokens, width), cotangent.reshape(tokens, width), peers)
    grads = group_backward(exchange(sent), qkv_weight, out_weight, tokens)
    input_grad, qkv_weight_grad, out_weight_grad = finish(exchange(grads), tokens, width)
    return (input_grad.reshape(rows_dev, cols_dev, width), qkv_weight_grad, out_weight_grad)


def solution(mesh):
    return jax.shard_map(
        local,
        mesh=mesh,
        in_specs=(P(("scene", "row"), "col", None), P(("scene", "row"), "col", None), P(), P()),
        out_specs=(
            P(("scene", "row"), "col", None),
            P(("scene", "row", "col"), None),
            P(("scene", "row", "col"), None),
        ),
        check_vma=False,
    )
```

time: 490 us -> 183 us (0.37); the launches traced: 483 us -> 183 us
  waiting for transfers between devices: 164 us -> 0 us
  local copies, waits for them, and re-layouts: 141 us -> 2.53 us
  blocking collectives: 31.3 us -> 119 us
  matrix products: 60.5 us -> 0 us
  Pallas kernels: 0 us -> 60.2 us
  other arithmetic: 43.6 us -> 0 us
  starting transfers between devices: 26.7 us -> 0 us
  between operations: 15.4 us -> 0.65 us
    unnamed x2 -> x0, waiting for transfers between devices: 102 us -> none
    all_to_all x1 -> x2, blocking collectives: 31.3 us -> 119 us  [the longest x1 75 us: local(): exchange(grads)]
    all_to_all x5 -> x0, waiting for transfers between devices: 62.5 us -> none  [the longest x1 22.1 us: local(): lax.all_to_all(lax.all_to_all(grad_block, 'row', split_axis=0, concat_axi...]
    dot_general x11 -> x0, matrix products: 60.5 us -> none  [the longest x1 11.8 us: backward_pass(): jnp.einsum('nqhd,nkhd->nhqk', out_grad, value_rows, preferred_element_typ...]
    pallas_call x0 -> x3, Pallas kernels: none -> 60.2 us  [the longest x1 56.7 us: group_backward(): pl.pallas_call(main_kernel, in_specs=[vmem] * 3, out_specs=vmem, out_shap...]
    reshape x10 -> x0, local copies, waits for them, and re-layouts: 49.2 us -> none  [the longest x1 16.4 us: forward_pass(): projected.reshape(element_count, sequence_length, 3, HEADS, head_dim)]
    convert_element_type x4 -> x0, local copies, waits for them, and re-layouts: 39.9 us -> none  [the longest x3 35 us: backward_pass(): jnp.stack([query_grad, key_grad, value_grad], axis=2).astype(jnp.bfloat16)]
    all_to_all x5 -> x0, starting transfers between devices: 26.6 us -> none  [the longest x1 7.65 us: local(): lax.all_to_all(lax.all_to_all(arrange(activations), 'row', split_axis=0,...]
  transfers between devices with their start and end apart: 6 -> 0, of which waited for: 5 -> 0; matrix products, arithmetic and copies ran while one was open for 23% -> 0% of each run, Pallas kernels for 0% -> 0%
where the time goes in v1:
time: 183 us
  blocking collectives  119 us (65%)
  Pallas kernels  60.2 us (33%)
  local copies, waits for them, and re-layouts  2.53 us (1%)
    all_to_all x1, blocking collectives, local(): exchange(grads)  75 us
    pallas_call x1, Pallas kernels, group_backward(): pl.pallas_call(main_kernel, in_specs=[vmem] * 3, out_specs=vmem, out_shap...  56.7 us
    all_to_all x1, blocking collectives, local(): grads = group_backward(exchange(sent), qkv_weight, out_weight, tokens)  44.4 us

profile of v1, /device:TPU:0, one launch (start us, length us, event | category | flops | bytes accessed | tf_op | source)
XLA Modules:
  0.0 182.8 jit_solution(7038190259489591496)
XLA Ops:
  0.6 0.0 copy-start
  0.6 1.3 copy-done
  1.9 0.0 copy-start.1
  1.9 1.3 copy-done.1
  3.2 1.0 pack_tokens.1
  4.2 44.4 %all_to_all.22 = bf16[64,8,2304]{2,1,0:T(8,128)(2,1)} all-to-all(bf16[64,8,2304]{2,1,0:T(8,128)(2,1)S(1)} %bitcast.8), channel_id=1, replica_groups=mesh['scene'=2,'row'=8,'col'=8] {'row','col'}, dimensions={0} | all-to-all | bytes 4718592 | tf_op jit(solution)/shard_map/all_to_all | solution.py:299
  48.6 56.7 %group_backward.1 = bf16[512,5760]{1,0:T(8,128)(2,1)} custom-call(bf16[512,2304]{1,0:T(8,128)(2,1)} %bitcast.14, bf16[768,2304]{1,0:T(8,128)(2,1)} %qkv_w.1, bf16[768,768]{1,0:T(8,128)(2,1)} %out_w.1), custom_call_target="tpu_custom_call" | custom-call | tf_op jit(solution)/shard_map/group_backward/pallas_call | solution.py:231
  105.3 75.0 %all_to_all.23 = bf16[64,8,5760]{2,1,0:T(8,128)(2,1)S(1)} all-to-all(bf16[64,8,5760]{2,1,0:T(8,128)(2,1)} %bitcast.13), channel_id=1, replica_groups=mesh['scene'=2,'row'=8,'col'=8] {'row','col'}, dimensions={0} | all-to-all | bytes 11796480 | tf_op jit(solution)/shard_map/all_to_all | solution.py:300
  180.3 2.5 %finish.1 = (bf16[768,768]{1,0:T(8,128)(2,1)}, f32[12,2304]{1,0:T(8,128)}, f32[12,768]{1,0:T(8,128)}) custom-call(bf16[512,5760]{1,0:T(8,128)(2,1)S(1)} %bitcast.7), custom_call_target="tpu_custom_call" | custom-call | tf_op jit(solution)/shard_map/finish/pallas_call | solution.py:279
Async XLA Ops:
  0.6 1.3 copy-start
  1.9 1.3 copy-start.1

commit v2 on v1

--- a/solution.py
+++ b/solution.py
@@ -87,7 +87,7 @@
         to[main:, :half] = tail[:rest]
         to[main:, half:] = tail[rest:]
 
-    @pl.loop(0, tokens // seq)
+    @pl.loop(0, tokens // seq, unroll=4)
     def _(g):
         rows = pl.ds(pl.multiple_of(g * seq, seq), seq)
         x = xs[rows, :].astype(F32)
@@ -98,12 +98,12 @@
         mean_s[rows, :] = jnp.broadcast_to(mean, (seq, 128))
         inv_s[rows, :] = jnp.broadcast_to(inv, (seq, 128))
 
-    @pl.loop(0, 3 * width // 256)
+    @pl.loop(0, 3 * width // 256, unroll=3)
     def _(j):
         cols = pl.ds(pl.multiple_of(j * 256, 256), 256)
         qkv[:, cols] = nn(ns[...], qkv_w[:, cols]).astype(BF16)
 
-    @pl.loop(0, width // 256)
+    @pl.loop(0, width // 256, unroll=3)
     def _(j):
         cols = pl.ds(pl.multiple_of(j * 256, 256), 256)
         og[:, cols] = nt(cs[...], out_w[cols, :]).astype(BF16)
@@ -124,34 +124,41 @@
             total = jnp.where(lane_head == h, x[h * seq : (h + 1) * seq], total)
         return total
 
-    @pl.loop(0, tokens // seq)
+    @pl.loop(0, tokens // seq, unroll=2)
     def _(g):
         rows = pl.ds(pl.multiple_of(g * seq, seq), seq)
-        for c in range(0, width, lanes):
-            q = qkv[rows, c : c + lanes]
-            k = qkv[rows, width + c : width + c + lanes]
-            v = qkv[rows, 2 * width + c : 2 * width + c + lanes]
-            q_wide = spread(q)
-            g_wide = spread(og[rows, c : c + lanes])
-            scores = nt(k, q_wide)
-            top = jnp.max(scores, axis=0, keepdims=True)
-            e = jnp.exp((scores - top) * scaling)
+        blocks = range(0, width, lanes)
+        queries = [qkv[rows, c : c + lanes] for c in blocks]
+        keys = [qkv[rows, width + c : width + c + lanes] for c in blocks]
+        values = [qkv[rows, 2 * width + c : 2 * width + c + lanes] for c in blocks]
+        q_wide = [spread(q) for q in queries]
+        g_wide = [spread(og[rows, c : c + lanes]) for c in blocks]
+        scores = [nt(k, q) for k, q in zip(keys, q_wide)]
+        prob_grads = [nt(v, g) for v, g in zip(values, g_wide)]
+        probs_low, score_low = [], []
+        for score, prob_grad in zip(scores, prob_grads):
+            top = jnp.max(score, axis=0, keepdims=True)
+            e = jnp.exp((score - top) * scaling)
             probs = e * (1.0 / jnp.sum(e, axis=0, keepdims=True))
-            probs_low = probs.astype(BF16)
-            prob_grad = nt(v, g_wide)
             delta = jnp.sum(probs * prob_grad, axis=0, keepdims=True)
-            score_low = (probs * (prob_grad - delta)).astype(BF16)
-            att[rows, c : c + lanes] = fold(tn(probs_low, v)).astype(BF16)
-            dqkv[rows, c : c + lanes] = (fold(tn(score_low, k)) * scaling).astype(BF16)
-            dqkv[rows, width + c : width + c + lanes] = (nn(score_low, q_wide) * scaling).astype(BF16)
-            dqkv[rows, 2 * width + c : 2 * width + c + lanes] = nn(probs_low, g_wide).astype(BF16)
-
-    @pl.loop(0, width // 256)
+            probs_low.append(probs.astype(BF16))
+            score_low.append((probs * (prob_grad - delta)).astype(BF16))
+        value_grads = [nn(p, g) for p, g in zip(probs_low, g_wide)]
+        key_grads = [nn(s, q) for s, q in zip(score_low, q_wide)]
+        attended = [tn(p, v) for p, v in zip(probs_low, values)]
+        query_grads = [tn(s, k) for s, k in zip(score_low, keys)]
+        for i, c in enumerate(blocks):
+            dqkv[rows, width + c : width + c + lanes] = (key_grads[i] * scaling).astype(BF16)
+            dqkv[rows, 2 * width + c : 2 * width + c + lanes] = value_grads[i].astype(BF16)
+            att[rows, c : c + lanes] = fold(attended[i]).astype(BF16)
+            dqkv[rows, c : c + lanes] = (fold(query_grads[i]) * scaling).astype(BF16)
+
+    @pl.loop(0, width // 256, unroll=3)
     def _(j):
         cols = pl.ds(pl.multiple_of(j * 256, 256), 256)
         ngs[:, cols] = nt(dqkv[...], qkv_w[cols, :])
 
-    @pl.loop(0, tokens // seq)
+    @pl.loop(0, tokens // seq, unroll=4)
     def _(g):
         rows = pl.ds(pl.multiple_of(g * seq, seq), seq)
         inv = inv_s[rows, :][:, :1]
@@ -174,13 +181,13 @@
     at1[...] = nt(eight, att[...]).astype(BF16)
     at2[...] = nt(four, att[...]).astype(BF16)
 
-    @pl.loop(0, 3 * width // 256)
+    @pl.loop(0, 3 * width // 256, unroll=3)
     def _(j):
         cols = pl.ds(pl.multiple_of(j * 256, 256), 256)
         to = pl.ds(pl.multiple_of(packed + j * 256, 128), 256)
         out[:, to] = nn(nt1[...], dqkv[:, cols]).astype(BF16)
 
-    @pl.loop(0, width // 256)
+    @pl.loop(0, width // 256, unroll=3)
     def _(j):
         cols = pl.ds(pl.multiple_of(j * 256, 256), 256)
         to = pl.ds(pl.multiple_of(packed + 3 * width + j * 256, 128), 256)
@@ -189,7 +196,7 @@
     first = packed + 4 * width
     is_upper = lax.broadcasted_iota(jnp.int32, (main, 256), 0) % 8 < 4
 
-    @pl.loop(0, width // 256)
+    @pl.loop(0, width // 256, unroll=3)
     def _(j):
         a = pl.ds(pl.multiple_of(j * 256, 256), 256)
         b = pl.ds(pl.multiple_of(2 * width + j * 256, 256), 256)
@@ -197,7 +204,7 @@
         pair = jnp.where(is_upper, nn(nt2[...], dqkv[:, a]), nn(nt2[...], dqkv[:, b]))
         out[:, to] = pair.astype(BF16)
 
-    @pl.loop(0, width // 256)
+    @pl.loop(0, width // 256, unroll=3)
     def _(j):
         a = pl.ds(pl.multiple_of(width + j * 256, 256), 256)
         b = pl.ds(pl.multiple_of(j * 256, 256), 256)
@@ -234,7 +241,7 @@
         out_specs=vmem,
         out_shape=jax.ShapeDtypeStruct((main, 3 * width // 2 + 6 * width), BF16),
         scratch_shapes=scratch,
-        compiler_params=pltpu.CompilerParams(vmem_limit_bytes=56 * MIB),
+        compiler_params=pltpu.CompilerParams(vmem_limit_bytes=38 * MIB),
         name="group_backward",
     )(got, qkv_weight, out_weight)
 

time: 183 us -> 158 us (0.86)
  Pallas kernels: 60.2 us -> 35.2 us
    pallas_call x1, Pallas kernels: 56.7 us -> 31.7 us  [group_backward(): pl.pallas_call(main_kernel, in_specs=[vmem] * 3, out_specs=vmem, out_shap...]
where the time goes in v2:
time: 158 us
  blocking collectives  119 us (75%)
  Pallas kernels  35.2 us (22%)
  local copies, waits for them, and re-layouts  2.55 us (2%)
    all_to_all x1, blocking collectives, local(): exchange(grads)  74.8 us
    all_to_all x1, blocking collectives, local(): grads = group_backward(exchange(sent), qkv_weight, out_weight, tokens)  44.6 us
    pallas_call x1, Pallas kernels, group_backward(): pl.pallas_call(main_kernel, in_specs=[vmem] * 3, out_specs=vmem, out_shap...  31.7 us

profile of v2, /device:TPU:0, one launch (start us, length us, event | category | flops | bytes accessed | tf_op | source)
XLA Modules:
  0.0 157.7 jit_solution(14149695218619259610)
XLA Ops:
  0.6 0.0 copy-start
  0.6 1.3 copy-done
  1.9 0.0 copy-start.1
  1.9 1.3 copy-done.1
  3.2 1.0 pack_tokens.1
  4.2 0.0 copy-start.2
  4.2 0.0 copy-start.3
  4.2 44.6 %all_to_all.22 = bf16[64,8,2304]{2,1,0:T(8,128)(2,1)S(1)} all-to-all(bf16[64,8,2304]{2,1,0:T(8,128)(2,1)S(1)} %bitcast.10), channel_id=1, replica_groups=mesh['scene'=2,'row'=8,'col'=8] {'row','col'}, dimensions={0} | all-to-all | bytes 4718592 | tf_op jit(solution)/shard_map/all_to_all | solution.py:306
  48.8 0.0 copy-done.2
  48.8 0.0 copy-done.3
  48.8 31.7 %group_backward.1 = bf16[512,5760]{1,0:T(8,128)(2,1)S(1)} custom-call(bf16[512,2304]{1,0:T(8,128)(2,1)S(1)} %bitcast.9, bf16[768,2304]{1,0:T(8,128)(2,1)S(1)} %copy-done.2, bf16[768,768]{1,0:T(8,128)(2,1)S(1)} %copy-done.3), custom_call_target="tpu_custom_call" | custom-call | tf_op jit(solution)/shard_map/group_backward/pallas_call | solution.py:238
  80.5 74.8 %all_to_all.23 = bf16[64,8,5760]{2,1,0:T(8,128)(2,1)S(1)} all-to-all(bf16[64,8,5760]{2,1,0:T(8,128)(2,1)S(1)} %bitcast.8), channel_id=1, replica_groups=mesh['scene'=2,'row'=8,'col'=8] {'row','col'}, dimensions={0} | all-to-all | bytes 11796480 | tf_op jit(solution)/shard_map/all_to_all | solution.py:307
  155.2 2.5 %finish.1 = (bf16[768,768]{1,0:T(8,128)(2,1)}, f32[12,2304]{1,0:T(8,128)}, f32[12,768]{1,0:T(8,128)}) custom-call(bf16[512,5760]{1,0:T(8,128)(2,1)S(1)} %bitcast.7), custom_call_target="tpu_custom_call" | custom-call | tf_op jit(solution)/shard_map/finish/pallas_call | solution.py:286
Async XLA Ops:
  0.6 1.3 copy-start
  1.9 1.3 copy-start.1
  4.2 44.6 %copy-start.2 = (bf16[768,2304]{1,0:T(8,128)(2,1)S(1)}, bf16[768,2304]{1,0:T(8,128)(2,1)}, u32[]{:S(2)}) copy-start(bf16[768,2304]{1,0:T(8,128)(2,1)} %qkv_w.1) | copy-start | bytes 10616836
  4.2 44.6 %copy-start.3 = (bf16[768,768]{1,0:T(8,128)(2,1)S(1)}, bf16[768,768]{1,0:T(8,128)(2,1)}, u32[]{:S(2)}) copy-start(bf16[768,768]{1,0:T(8,128)(2,1)} %out_w.1) | copy-start | bytes 3538948

commit v3 on v1

v3 whole, which is shorter than its diff:
```python
import functools

import jax
import jax.numpy as jnp
from jax import lax
from jax.experimental import pallas as pl
from jax.experimental.pallas import tpu as pltpu
from jax.sharding import PartitionSpec as P

HEADS = 24
EPSILON = 1e-05
BF16 = jnp.bfloat16
F32 = jnp.float32
MIB = 1 << 20


SEQ = 64
LANES = 128
PAIRS = (("row", 2, 4, 2), ("row", 6, 5, 2), ("row", 1, 3, 2), ("col", 2, 1, 2), ("col", 6, 2, 1))
TILE = 256


def dot(a, b, dims):
    return lax.dot_general(a, b, ((dims[0], dims[1]), ((), ())), preferred_element_type=F32)


def nn(a, b):
    return dot(a, b, ((1,), (0,)))


def nt(a, b):
    return dot(a, b, ((1,), (1,)))


def tn(a, b):
    return dot(a, b, ((0,), (0,)))


def one_hot(shape, column_of_row):
    rows = lax.broadcasted_iota(jnp.int32, shape, 0)
    columns = lax.broadcasted_iota(jnp.int32, shape, 1)
    return jnp.where(columns == column_of_row(rows), 1.0, 0.0).astype(BF16)


def pack_kernel(act_main, act_tail, cot_main, cot_tail, out):
    rows, width = act_main.shape
    half = width // 2
    upper = one_hot((rows, rows // 2), lambda i: jnp.where(i % 8 < 4, (i // 8) * 4 + i % 4, -1))
    lower = one_hot((rows, rows // 2), lambda i: jnp.where(i % 8 < 4, -1, (i // 8) * 4 + i % 4))
    at = 0
    for main, tail in ((act_main, act_tail), (cot_main, cot_tail)):
        out[:, at : at + width] = main[...]
        packed = nn(upper, tail[:, :half]) + nn(lower, tail[:, half:])
        out[:, at + width : at + width + half] = packed.astype(BF16)
        at += width + half


def pack_tokens(act, cot, peers):
    tokens, width = act.shape
    steps = 4
    rows = peers * 8 // steps
    main = pl.BlockSpec((rows, width), lambda i: (i, 0))
    tail = pl.BlockSpec((rows // 2, width), lambda i: (2 * steps + i, 0))
    return pl.pallas_call(
        pack_kernel,
        grid=(steps,),
        in_specs=[main, tail, main, tail],
        out_specs=pl.BlockSpec((rows, 3 * width), lambda i: (i, 0)),
        out_shape=jax.ShapeDtypeStruct((peers * 8, 3 * width), BF16),
        compiler_params=pltpu.CompilerParams(vmem_limit_bytes=32 * MIB),
        name="pack_tokens",
    )(act, act, cot, cot)


def parameters(limit, flops=0, moved=0):
    return dict(
        compiler_params=pltpu.CompilerParams(vmem_limit_bytes=limit * MIB),
        cost_estimate=pl.CostEstimate(flops=flops, bytes_accessed=moved, transcendentals=0),
    )


def rows_of(g):
    return pl.ds(pl.multiple_of(g * SEQ, SEQ), SEQ)


def project(ns, cs, qkv_w, out_w, qkv, og):
    for c in range(0, qkv.shape[1], 256):
        qkv[:, c : c + 256] = nn(ns[...], qkv_w[:, c : c + 256]).astype(BF16)
    for c in range(0, og.shape[1], 256):
        og[:, c : c + 256] = nt(cs[...], out_w[c : c + 256, :]).astype(BF16)


def attend(qkv, og, dqkv, att, together):
    tokens, count = og.shape
    head_dim = 32
    scaling = head_dim**-0.5
    heads = LANES // head_dim
    shape = (heads * SEQ, LANES)
    own = lax.broadcasted_iota(jnp.int32, shape, 0) // SEQ
    keep = jnp.where(lax.broadcasted_iota(jnp.int32, shape, 1) // head_dim == own, 1.0, 0.0).astype(BF16)
    lane_head = lax.broadcasted_iota(jnp.int32, (SEQ, LANES), 1) // head_dim

    def spread(x):
        return jnp.concatenate([x] * heads, axis=0) * keep

    def fold(x):
        total = x[:SEQ]
        for h in range(1, heads):
            total = jnp.where(lane_head == h, x[h * SEQ : (h + 1) * SEQ], total)
        return total

    @pl.loop(0, tokens // SEQ // together)
    def _(step):
        blocks = [(rows_of(step * together + g), c) for g in range(together) for c in range(0, count, LANES)]
        queries = [qkv[rows, c : c + LANES] for rows, c in blocks]
        keys = [qkv[rows, count + c : count + c + LANES] for rows, c in blocks]
        values = [qkv[rows, 2 * count + c : 2 * count + c + LANES] for rows, c in blocks]
        q_wide = [spread(q) for q in queries]
        g_wide = [spread(og[rows, c : c + LANES]) for rows, c in blocks]
        scores = [nt(k, q) for k, q in zip(keys, q_wide)]
        prob_grads = [nt(v, g) for v, g in zip(values, g_wide)]
        probs_low, score_low = [], []
        for score, prob_grad in zip(scores, prob_grads):
            top = jnp.max(score, axis=0, keepdims=True)
            e = jnp.exp((score - top) * scaling)
            probs = e * (1.0 / jnp.sum(e, axis=0, keepdims=True))
            delta = jnp.sum(probs * prob_grad, axis=0, keepdims=True)
            probs_low.append(probs.astype(BF16))
            score_low.append((probs * (prob_grad - delta)).astype(BF16))
        value_grads = [nn(p, g) for p, g in zip(probs_low, g_wide)]
        key_grads = [nn(s, q) for s, q in zip(score_low, q_wide)]
        attended = [tn(p, v) for p, v in zip(probs_low, values)]
        query_grads = [tn(s, k) for s, k in zip(score_low, keys)]
        for i, (rows, c) in enumerate(blocks):
            dqkv[rows, count + c : count + c + LANES] = (key_grads[i] * scaling).astype(BF16)
            dqkv[rows, 2 * count + c : 2 * count + c + LANES] = value_grads[i].astype(BF16)
            att[rows, c : c + LANES] = fold(attended[i]).astype(BF16)
            dqkv[rows, c : c + LANES] = (fold(query_grads[i]) * scaling).astype(BF16)


def eight_rows(shape):
    return one_hot(shape, lambda i: (i // 8) * 12 + i % 8)


def four_rows(shape):
    return one_hot(shape, lambda i: (i // 8) * 12 + 8 + i % 4)


def main_kernel(
    bits, got, qkv_w, out_w, xs, cs, stats, dqkv, *refs
):
    kept, sent = refs[: len(PAIRS)], refs[len(PAIRS) : 2 * len(PAIRS)]
    ns, nt1, nt2, at1, at2, att, qkv, og, order = refs[2 * len(PAIRS) :]
    width = out_w.shape[0]
    half = width // 2
    tokens = xs.shape[0]
    main = got.shape[0]
    rest = tokens - main
    packed = width + half

    order[...] = one_hot((main, main), lambda k: (k % SEQ) * 8 + k // SEQ)
    for first, to in ((0, xs), (packed, cs)):
        for c in range(0, width, half):
            to[:main, c : c + half] = nn(order[...], got[:, first + c : first + c + half]).astype(BF16)
        tail = nn(order[...], got[:, first + width : first + packed]).astype(BF16)
        to[main:, :half] = tail[:rest]
        to[main:, half:] = tail[rest:]

    @pl.loop(0, tokens // SEQ, unroll=4)
    def _(g):
        rows = rows_of(g)
        x = xs[rows, :].astype(F32)
        mean = jnp.mean(x, axis=-1, keepdims=True)
        centred = x - mean
        inv = lax.rsqrt(jnp.mean(centred * centred, axis=-1, keepdims=True) + EPSILON)
        ns[rows, :] = (centred * inv).astype(BF16)
        stats[rows, :LANES] = jnp.broadcast_to(mean, (SEQ, LANES))
        stats[rows, LANES:] = jnp.broadcast_to(inv, (SEQ, LANES))

    project(ns, cs, qkv_w, out_w, qkv, og)
    attend(qkv, og, dqkv, att, 2)

    eight, four = eight_rows((main, width)), four_rows((main, width))
    for pick, source, to in ((eight, ns, nt1), (four, ns, nt2), (eight, att, at1), (four, att, at2)):
        to[...] = nt(pick, source[...]).astype(BF16)
    tile = TILE
    shape = (main, tile)
    place = lax.broadcasted_iota(jnp.int32, shape, 0)
    is_upper = place % 8 < 4

    def share(keep, send, c, low, high, direction):
        same = (place // (8 << PAIRS[direction][2])) % 2 == bits[direction]
        keep[:, c : c + tile] = jnp.where(same, low, high).astype(BF16)
        send[:, c : c + tile] = jnp.where(same, high, low).astype(BF16)

    places = [(i, c) for i, pair in enumerate(PAIRS) for c in range(0, pair[3] * tile, tile)]
    for c in range(0, width, tile):
        q, k, v = (slice(part * width + c, part * width + c + tile) for part in range(3))
        for kind in range(3):
            if kind == 0:
                low, high = nn(nt1[...], dqkv[:, q]), nn(nt1[...], dqkv[:, k])
            elif kind == 1:
                low, high = nn(nt1[...], dqkv[:, v]), nn(at1[...], cs[:, q])
            else:
                low = jnp.where(is_upper, nn(nt2[...], dqkv[:, q]), nn(nt2[...], dqkv[:, v]))
                high = jnp.where(is_upper, nn(nt2[...], dqkv[:, k]), nn(at2[...], cs[:, q]))
            direction, to = places[kind * (width // tile) + c // tile]
            share(kept[direction], sent[direction], to, low, high, direction)


def main_part(bits, got, qkv_weight, out_weight, tokens):
    width = out_weight.shape[0]
    main = got.shape[0]
    vmem = pl.BlockSpec(memory_space=pltpu.VMEM)
    square = (tokens, width)
    outs = [(square, BF16), (square, BF16), ((tokens, 2 * LANES), F32), ((tokens, 3 * width), BF16)]
    outs += [((main, pair[3] * TILE), BF16) for pair in PAIRS * 2]
    return pl.pallas_call(
        main_kernel,
        in_specs=[pl.BlockSpec(memory_space=pltpu.SMEM)] + [vmem] * 3,
        out_specs=[vmem] * len(outs),
        out_shape=[jax.ShapeDtypeStruct(s, d) for s, d in outs],
        scratch_shapes=[pltpu.VMEM(square, BF16)]
        + [pltpu.VMEM((main, tokens), BF16)] * 4
        + [
            pltpu.VMEM(square, BF16),
            pltpu.VMEM((tokens, 3 * width), BF16),
            pltpu.VMEM(square, BF16),
            pltpu.VMEM((main, main), BF16),
        ],
        name="main_part",
        **parameters(34, 16 * 10**9, 30 * 10**6),
    )(bits, got, qkv_weight, out_weight)


def token_kernel(xs, cs, stats, dqkv, qkv_w, out, ngs, igs):
    tokens, width = xs.shape
    main = out.shape[0]
    rest = tokens - main
    half = width // 2
    for f in range(0, width, 256):
        ngs[:, f : f + 256] = nt(dqkv[...], qkv_w[f : f + 256, :])

    @pl.loop(0, tokens // SEQ, unroll=4)
    def _(g):
        rows = rows_of(g)
        inv = stats[rows, LANES:][:, :1]
        xhat = (xs[rows, :].astype(F32) - stats[rows, :LANES][:, :1]) * inv
        ng = ngs[rows, :]
        centred = ng - jnp.mean(ng, axis=-1, keepdims=True)
        centred = centred - xhat * jnp.mean(ng * xhat, axis=-1, keepdims=True)
        igs[rows, :] = (cs[rows, :].astype(F32) + inv * centred).astype(BF16)

    back = one_hot((main, main), lambda i: (i % 8) * SEQ + i // 8)
    for c in range(0, width, half):
        out[:, c : c + half] = nn(back, igs[:main, c : c + half]).astype(BF16)
    tail = nn(back[:, :rest], igs[main:, :half]) + nn(back[:, rest:], igs[main:, half:])
    out[:, width:] = tail.astype(BF16)


def token_part(xs, cs, stats, dqkv, qkv_weight, main):
    tokens, width = xs.shape
    vmem = pl.BlockSpec(memory_space=pltpu.VMEM)
    return pl.pallas_call(
        token_kernel,
        in_specs=[vmem] * 5,
        out_specs=vmem,
        out_shape=jax.ShapeDtypeStruct((main, width + width // 2), BF16),
        scratch_shapes=[pltpu.VMEM((tokens, width), F32), pltpu.VMEM((tokens, width), BF16)],
        name="token_grad",
        **parameters(20, 4 * 10**9, 12 * 10**6),
    )(xs, cs, stats, dqkv, qkv_weight)


def join_kernel(grad, *refs):
    *pairs, out = refs
    at = grad.shape[1]
    out[:, :at] = grad[...]
    for keep, came in zip(pairs[: len(PAIRS)], pairs[len(PAIRS) :], strict=True):
        count = keep.shape[1]
        out[:, at : at + count] = (keep[...].astype(F32) + came[...].astype(F32)).astype(BF16)
        at += count


def join(grad, pairs):
    rows = grad.shape[0]
    arrays = [grad, *pairs]
    width = grad.shape[1] + sum(a.shape[1] for a in pairs) // 2
    block = lambda count: pl.BlockSpec((rows // 4, count), lambda i: (i, 0))
    return pl.pallas_call(
        join_kernel,
        grid=(4,),
        in_specs=[block(a.shape[1]) for a in arrays],
        out_specs=block(width),
        out_shape=jax.ShapeDtypeStruct((rows, width), BF16),
        name="join",
        **parameters(16, 0, 8 * 10**6),
    )(*arrays)


def finish_kernel(bits, got, grad, qkv_grad, out_grad, total):
    step = pl.program_id(0)
    rows = got.shape[0]
    width = grad.shape[1]
    half = width // 2
    packed = width + half
    main = 8 * grad.shape[0] // 12
    grad[pl.ds(pl.multiple_of(step * rows, 16), rows), :] = got[:, :width]
    pick = one_hot((rows // 2, rows), lambda k: (k // 4) * 8 + k % 4)
    pick_low = one_hot((rows // 2, rows), lambda k: (k // 4) * 8 + 4 + k % 4)
    tail = pl.ds(pl.multiple_of(main + step * (rows // 2), 16), rows // 2)
    grad[tail, :half] = nn(pick, got[:, width:packed]).astype(BF16)
    grad[tail, half:] = nn(pick_low, got[:, width:packed]).astype(BF16)

    @pl.when(step == 0)
    def _():
        total[...] = jnp.zeros_like(total)

    blocks = width // TILE
    places = [i for i, pair in enumerate(PAIRS) for _ in range(pair[3])]
    for block, direction in enumerate(places):
        first = packed + block * TILE
        came = got[:, first : first + TILE].astype(F32)
        bit = PAIRS[direction][2]
        if rows <= 8 << bit:
            every = came.reshape(-1, 8, TILE).sum(axis=0)
            odd = (step * rows // (8 << bit)) % 2 == 1
            low, high = jnp.where(odd, 0.0, every), jnp.where(odd, every, 0.0)
        else:
            runs = came.reshape(-1, 8 << bit, TILE)
            low = sum(runs[i].reshape(-1, 8, TILE).sum(axis=0) for i in range(0, runs.shape[0], 2))
            high = sum(runs[i].reshape(-1, 8, TILE).sum(axis=0) for i in range(1, runs.shape[0], 2))
        at = (2 * (block // blocks) * blocks + block % blocks) * TILE
        total[:, at : at + TILE] += jnp.where(bits[direction] == 0, low, high)
        total[:, at + width : at + width + TILE] += jnp.where(bits[direction] == 0, high, low)

    @pl.when(step == pl.num_programs(0) - 1)
    def _():
        q, k, v, o, low, high = (total[:, i * width : (i + 1) * width] for i in range(6))
        for part, (top, end) in enumerate(((q, low[:4]), (k, high[:4]), (v, low[4:]))):
            qkv_grad[:8, part * width : (part + 1) * width] = top
            qkv_grad[8:12, part * width : (part + 1) * width] = end
        out_grad[:8, :] = o
        out_grad[8:12, :] = high[4:]


def finish(bits, got, tokens, width):
    steps = 4
    rows = got.shape[0] // steps
    whole = lambda shape: pl.BlockSpec(shape, lambda i: (0, 0))
    shapes = ((tokens, width), (12, 3 * width), (12, width))
    return pl.pallas_call(
        finish_kernel,
        grid=(steps,),
        in_specs=[pl.BlockSpec(memory_space=pltpu.SMEM), pl.BlockSpec((rows, got.shape[1]), lambda i: (i, 0))],
        out_specs=[whole(s) for s in shapes],
        out_shape=[jax.ShapeDtypeStruct(s, d) for s, d in zip(shapes, (BF16, F32, F32), strict=True)],
        scratch_shapes=[pltpu.VMEM((8, 6 * width), F32)],
        name="finish",
        **parameters(24, 10**9, 5 * 10**6),
    )(bits, got)


def local(activations, cotangent, qkv_weight, out_weight):
    grid_rows, grid_cols = lax.axis_size("row"), lax.axis_size("col")
    peers = grid_rows * grid_cols
    rows_dev, cols_dev, width = activations.shape
    tokens = rows_dev * cols_dev
    exchange = functools.partial(
        lax.all_to_all, axis_name=("row", "col"), split_axis=0, concat_axis=0, tiled=True
    )
    row, col = lax.axis_index("row"), lax.axis_index("col")
    place = row * grid_cols + col
    bits = jnp.stack([place // (1 << bit) % 2 for _, _, bit, _ in PAIRS]).astype(jnp.int32)
    sent = pack_tokens(activations.reshape(tokens, width), cotangent.reshape(tokens, width), peers)
    sent, bits = lax.optimization_barrier((sent, bits))
    xs, cs, stats, dqkv, *pairs = main_part(bits, exchange(sent), qkv_weight, out_weight, tokens)
    came = [
        lax.ppermute(x, axis, [(i, i ^ other) for i in range(lax.axis_size(axis))])
        for x, (axis, other, _, _) in zip(pairs[len(PAIRS) :], PAIRS, strict=True)
    ]
    grads = token_part(xs, cs, stats, dqkv, qkv_weight, peers * 8)
    got = exchange(join(grads, (*pairs[: len(PAIRS)], *came)))
    input_grad, qkv_weight_grad, out_weight_grad = finish(bits, got, tokens, width)
    return (input_grad.reshape(rows_dev, cols_dev, width), qkv_weight_grad, out_weight_grad)


def solution(mesh):
    return jax.shard_map(
        local,
        mesh=mesh,
        in_specs=(P(("scene", "row"), "col", None), P(("scene", "row"), "col", None), P(), P()),
        out_specs=(
            P(("scene", "row"), "col", None),
            P(("scene", "row", "col"), None),
            P(("scene", "row", "col"), None),
        ),
        check_vma=False,
    )
```

time: 183 us -> 139 us (0.76)
  blocking collectives: 119 us -> 93.2 us
  Pallas kernels: 60.2 us -> 35 us
  waiting for transfers between devices: 0 us -> 3.94 us
  starting transfers between devices: 0 us -> 3.48 us
    all_to_all x2, blocking collectives: 119 us -> 93.2 us  [the longest x1 48.6 us: local(): got = exchange(join(grads, (*pairs[:len(PAIRS)], *came)))]
    pallas_call x2 -> x4, Pallas kernels: 59.2 us -> 34 us  [the longest x1 23.4 us: main_part(): pl.pallas_call(main_kernel, in_specs=[pl.BlockSpec(memory_space=pltpu.SME...]
    ppermute x0 -> x5, waiting for transfers between devices: none -> 3.94 us  [local(): lax.ppermute(x, axis, [(i, i ^ other) for i in range(lax.axis_size(axis))])]
    ppermute x0 -> x5, starting transfers between devices: none -> 3.48 us  [local(): lax.ppermute(x, axis, [(i, i ^ other) for i in range(lax.axis_size(axis))])]
  transfers between devices with their start and end apart: 0 -> 5, of which waited for: 0 -> 4; matrix products, arithmetic and copies ran while one was open for 0% -> 0% of each run, Pallas kernels for 0% -> 5%
where the time goes in v3:
time: 139 us
  blocking collectives  93.2 us (67%)
  Pallas kernels  35 us (25%)
  waiting for transfers between devices  3.94 us (3%)
  starting transfers between devices  3.48 us (3%)
  local copies, waits for them, and re-layouts  2.63 us (2%)
    all_to_all x1, blocking collectives, local(): got = exchange(join(grads, (*pairs[:len(PAIRS)], *came)))  48.6 us
    all_to_all x1, blocking collectives, local(): exchange(sent)  44.5 us
    pallas_call x1, Pallas kernels, main_part(): pl.pallas_call(main_kernel, in_specs=[pl.BlockSpec(memory_space=pltpu.SME...  23.4 us
    pallas_call x1, Pallas kernels, token_part(): pl.pallas_call(token_kernel, in_specs=[vmem] * 5, out_specs=vmem, out_sha...  7.18 us
    ppermute x5, waiting for transfers between devices, local(): lax.ppermute(x, axis, [(i, i ^ other) for i in range(lax.axis_size(axis))])  3.94 us
    ppermute x5, starting transfers between devices, local(): lax.ppermute(x, axis, [(i, i ^ other) for i in range(lax.axis_size(axis))])  3.48 us
  transfers between devices with their start and end apart: 5, of which 4 were waited for; matrix products, arithmetic and copies ran while one was open for 0% of the time, Pallas kernels for 5%

profile of v3, /device:TPU:0, one launch (start us, length us, event | category | flops | bytes accessed | tf_op | source)
XLA Modules:
  0.0 139.0 jit_solution(12120539559773983073)
XLA Ops:
  0.7 0.0 copy-start
  0.8 1.3 copy-done
  2.0 0.0 copy-start.1
  2.0 1.3 copy-done.1
  3.3 1.0 pack_tokens.1
  4.3 0.1 stack.23.bits
  4.4 0.0 copy-start.2
  4.4 0.0 copy-start.3
  4.4 44.5 %all_to_all.22 = bf16[64,8,2304]{2,1,0:T(8,128)(2,1)S(1)} all-to-all(bf16[64,8,2304]{2,1,0:T(8,128)(2,1)S(1)} %bitcast.13), channel_id=1, replica_groups=mesh['scene'=2,'row'=8,'col'=8] {'row','col'}, dimensions={0} | all-to-all | bytes 4718592 | tf_op jit(solution)/shard_map/all_to_all | solution.py:377
  49.0 0.0 copy-done.2
  49.0 0.0 copy-done.3
  49.0 23.4 %main_part.1 = (bf16[768,768]{1,0:T(8,128)(2,1)S(1)}, bf16[768,768]{1,0:T(8,128)(2,1)S(1)}, f32[768,256]{1,0:T(8,128)S(1)}, bf16[768,2304]{1,0:T(8,128)(2,1)S(1)...) custom-call(s32[5]{0:T(128)S(1)} %stack.23.bits, ...), custom_call_target="tpu_custom_call" | custom-call | flops 16000000000 | bytes 30000000 | tf_op jit(solution)/shard_map/main_part/pallas_call | solution.py:218
  72.4 0.7 collective-permute-start
  73.1 1.2 collective-permute-start.1
  74.3 0.7 collective-permute-start.2
  75.0 0.5 collective-permute-start.3
  75.5 0.3 collective-permute-start.4
  75.8 7.2 %token_grad.1.grad = bf16[512,1152]{1,0:T(8,128)(2,1)S(1)} custom-call(bf16[768,768]{1,0:T(8,128)(2,1)S(1)} %get-tuple-element.24.xs, bf16[768,768]{1,0:T(8,128)(2,1)S(1)} %get-tuple-element.25.cs, f32[768,256]{1,0:T(8,128)S(1)} %get-tuple-element.26.stats, bf16[768,2304]{1,0:T(8,128)(2,1)S(1)} %get-tuple-element.27.dqkv, bf16[768,2304]{1,0:T(8,128)(2,1)S(1)} %copy-done.2), custom_call_target="tpu_custom_call" | custom-call | flops 4000000000 | bytes 12000000 | tf_op jit(solution)/shard_map/token_grad/pallas_call | solution.py:264
  83.0 0.1 collective-permute-done.4.refs_9_
  83.1 1.5 %collective-permute-done.refs_5_ = bf16[512,512]{1,0:T(8,128)(2,1)S(1)} collective-permute-done((bf16[512,512]{1,0:T(8,128)(2,1)S(1)}, bf16[512,512]{1,0:T(8,128)(2,1)S(1)}, u32[]{:S(2)}, u32[]{:S(2)}) %collective-permute-start) | collective-permute-done | bytes 524320 | tf_op jit(solution)/shard_map/ppermute | solution.py:379
  84.6 1.8 %collective-permute-done.1.refs_6_ = bf16[512,512]{1,0:T(8,128)(2,1)S(1)} collective-permute-done((bf16[512,512]{1,0:T(8,128)(2,1)S(1)}, bf16[512,512]{1,0:T(8,128)(2,1)S(1)}, u32[]{:S(2)}, u32[]{:S(2)}) %collective-permute-start.1) | collective-permute-done | bytes 524320 | tf_op jit(solution)/shard_map/ppermute | solution.py:379
  86.3 0.0 collective-permute-done.2.refs_7_
  86.3 0.6 collective-permute-done.3.refs_8_
  87.0 0.7 join.1
  87.6 48.6 %all_to_all.23 = bf16[64,8,3456]{2,1,0:T(8,128)(2,1)S(1)} all-to-all(bf16[64,8,3456]{2,1,0:T(8,128)(2,1)S(1)} %bitcast.12), channel_id=1, replica_groups=mesh['scene'=2,'row'=8,'col'=8] {'row','col'}, dimensions={0} | all-to-all | bytes 7077888 | tf_op jit(solution)/shard_map/all_to_all | solution.py:383
  136.3 2.8 %finish.1 = (bf16[768,768]{1,0:T(8,128)(2,1)}, f32[12,2304]{1,0:T(8,128)}, f32[12,768]{1,0:T(8,128)}) custom-call(s32[5]{0:T(128)S(1)} %stack.23.bits, bf16[512,3456]{1,0:T(8,128)(2,1)S(1)} %bitcast.18), custom_call_target="tpu_custom_call" | custom-call | flops 1000000000 | bytes 5000000 | tf_op jit(solution)/shard_map/finish/pallas_call | solution.py:352
Async XLA Ops:
  0.7 1.3 copy-start
  2.0 1.3 copy-start.1
  4.4 44.6 %copy-start.2 = (bf16[768,2304]{1,0:T(8,128)(2,1)S(1)}, bf16[768,2304]{1,0:T(8,128)(2,1)}, u32[]{:S(2)}) copy-start(bf16[768,2304]{1,0:T(8,128)(2,1)} %qkv_w.3) | copy-start | bytes 10616836
  4.4 44.6 %copy-start.3 = (bf16[768,768]{1,0:T(8,128)(2,1)S(1)}, bf16[768,768]{1,0:T(8,128)(2,1)}, u32[]{:S(2)}) copy-start(bf16[768,768]{1,0:T(8,128)(2,1)} %out_w.1) | copy-start | bytes 3538948
  72.4 12.2 %collective-permute-start = (bf16[512,512]{1,0:T(8,128)(2,1)S(1)}, bf16[512,512]{1,0:T(8,128)(2,1)S(1)}, u32[]{:S(2)}, u32[]{:S(2)}) collective-permute-start(bf16[512,512]{1,0:T(8,128)(2,1)S(1)} %get-tuple-element.33), channel_id=1, source_target_pairs={{0,16},{8,24},{16,0},{24,8},{32,48},{40,56},{48,32},{56,40},{1,17}... | collective-permute-start | bytes 1572872 | tf_op jit(solution)/shard_map/ppermute | solution.py:379
  73.1 13.2 %collective-permute-start.1 = (bf16[512,512]{1,0:T(8,128)(2,1)S(1)}, bf16[512,512]{1,0:T(8,128)(2,1)S(1)}, u32[]{:S(2)}, u32[]{:S(2)}) collective-permute-start(bf16[512,512]{1,0:T(8,128)(2,1)S(1)} %get-tuple-element.34), channel_id=1, source_target_pairs={{0,48},{8,56},{16,32},{24,40},{32,16},{40,24},{48,0},{56,8},{1,49}... | collective-permute-start | bytes 1572872 | tf_op jit(solution)/shard_map/ppermute | solution.py:379
  74.3 12.0 %collective-permute-start.2 = (bf16[512,512]{1,0:T(8,128)(2,1)S(1)}, bf16[512,512]{1,0:T(8,128)(2,1)S(1)}, u32[]{:S(2)}, u32[]{:S(2)}) collective-permute-start(bf16[512,512]{1,0:T(8,128)(2,1)S(1)} %get-tuple-element.35), channel_id=1, source_target_pairs={{0,8},{8,0},{16,24},{24,16},{32,40},{40,32},{48,56},{56,48},{1,9},... | collective-permute-start | bytes 1572872 | tf_op jit(solution)/shard_map/ppermute | solution.py:379
  75.0 12.0 %collective-permute-start.3 = (bf16[512,512]{1,0:T(8,128)(2,1)S(1)}, bf16[512,512]{1,0:T(8,128)(2,1)S(1)}, u32[]{:S(2)}, u32[]{:S(2)}) collective-permute-start(bf16[512,512]{1,0:T(8,128)(2,1)S(1)} %get-tuple-element.36), channel_id=1, source_target_pairs={{0,2},{1,3},{2,0},{3,1},{4,6},{5,7},{6,4},{7,5},{8,10},{9,11},{10,... | collective-permute-start | bytes 1572872 | tf_op jit(solution)/shard_map/ppermute | solution.py:379
  75.5 7.6 %collective-permute-start.4 = (bf16[512,256]{1,0:T(8,128)(2,1)S(1)}, bf16[512,256]{1,0:T(8,128)(2,1)S(1)}, u32[]{:S(2)}, u32[]{:S(2)}) collective-permute-start(bf16[512,256]{1,0:T(8,128)(2,1)S(1)} %get-tuple-element.37), channel_id=1, source_target_pairs={{0,6},{1,7},{2,4},{3,5},{4,2},{5,3},{6,0},{7,1},{8,14},{9,15},{10,... | collective-permute-start | bytes 786440 | tf_op jit(solution)/shard_map/ppermute | solution.py:379

commit v4 on v3

--- a/solution.py
+++ b/solution.py
@@ -16,7 +16,13 @@
 
 SEQ = 64
 LANES = 128
-PAIRS = (("row", 2, 4, 2), ("row", 6, 5, 2), ("row", 1, 3, 2), ("col", 2, 1, 2), ("col", 6, 2, 1))
+STREAMS = (
+    ((16, 4), (8, 3), 2),
+    ((48, 5), (2, 1), 2),
+    ((8, 3), (16, 4), 2),
+    ((2, 1), (48, 5), 2),
+    ((6, 2), (9, 0), 1),
+)
 TILE = 256
 
 
@@ -77,6 +83,10 @@
         compiler_params=pltpu.CompilerParams(vmem_limit_bytes=limit * MIB),
         cost_estimate=pl.CostEstimate(flops=flops, bytes_accessed=moved, transcendentals=0),
     )
+
+
+def is_own(row, bits, bit):
+    return (row // (8 << bit)) % 2 == bits[bit]
 
 
 def rows_of(g):
@@ -143,14 +153,15 @@
 
 
 def four_rows(shape):
-    return one_hot(shape, lambda i: (i // 8) * 12 + 8 + i % 4)
+    return one_hot(shape, lambda i: (i // 4) * 12 + 8 + i % 4)
 
 
 def main_kernel(
     bits, got, qkv_w, out_w, xs, cs, stats, dqkv, *refs
 ):
-    kept, sent = refs[: len(PAIRS)], refs[len(PAIRS) : 2 * len(PAIRS)]
-    ns, nt1, nt2, at1, at2, att, qkv, og, order = refs[2 * len(PAIRS) :]
+    count = len(STREAMS)
+    kept, sent = refs[:count], refs[count : 2 * count]
+    ns, nt1, nt2, at1, at2, att, qkv, og, order = refs[2 * count :]
     width = out_w.shape[0]
     half = width // 2
     tokens = xs.shape[0]
@@ -180,20 +191,26 @@
     project(ns, cs, qkv_w, out_w, qkv, og)
     attend(qkv, og, dqkv, att, 2)
 
-    eight, four = eight_rows((main, width)), four_rows((main, width))
+    eight, four = eight_rows((main, width)), four_rows((main // 2, width))
     for pick, source, to in ((eight, ns, nt1), (four, ns, nt2), (eight, att, at1), (four, att, at2)):
         to[...] = nt(pick, source[...]).astype(BF16)
     tile = TILE
     shape = (main, tile)
     place = lax.broadcasted_iota(jnp.int32, shape, 0)
-    is_upper = place % 8 < 4
+    is_upper = lax.broadcasted_iota(jnp.int32, (main // 16, 8, tile), 1) < 4
+
+    def under(a, b):
+        a, b = a.reshape(is_upper.shape), b.reshape(is_upper.shape)
+        first = jnp.where(is_upper, a, pltpu.roll(b, 4, 1))
+        second = jnp.where(is_upper, pltpu.roll(a, 4, 1), b)
+        return jnp.stack([first, second], axis=1).reshape(shape)
 
     def share(keep, send, c, low, high, direction):
-        same = (place // (8 << PAIRS[direction][2])) % 2 == bits[direction]
+        same = is_own(place, bits, STREAMS[direction][0][1])
         keep[:, c : c + tile] = jnp.where(same, low, high).astype(BF16)
         send[:, c : c + tile] = jnp.where(same, high, low).astype(BF16)
 
-    places = [(i, c) for i, pair in enumerate(PAIRS) for c in range(0, pair[3] * tile, tile)]
+    places = [(i, c) for i, pair in enumerate(STREAMS) for c in range(0, pair[2] * tile, tile)]
     for c in range(0, width, tile):
         q, k, v = (slice(part * width + c, part * width + c + tile) for part in range(3))
         for kind in range(3):
@@ -202,8 +219,8 @@
             elif kind == 1:
                 low, high = nn(nt1[...], dqkv[:, v]), nn(at1[...], cs[:, q])
             else:
-                low = jnp.where(is_upper, nn(nt2[...], dqkv[:, q]), nn(nt2[...], dqkv[:, v]))
-                high = jnp.where(is_upper, nn(nt2[...], dqkv[:, k]), nn(at2[...], cs[:, q]))
+                low = under(nn(nt2[...], dqkv[:, q]), nn(nt2[...], dqkv[:, v]))
+                high = under(nn(nt2[...], dqkv[:, k]), nn(at2[...], cs[:, q]))
             direction, to = places[kind * (width // tile) + c // tile]
             share(kept[direction], sent[direction], to, low, high, direction)
 
@@ -214,14 +231,14 @@
     vmem = pl.BlockSpec(memory_space=pltpu.VMEM)
     square = (tokens, width)
     outs = [(square, BF16), (square, BF16), ((tokens, 2 * LANES), F32), ((tokens, 3 * width), BF16)]
-    outs += [((main, pair[3] * TILE), BF16) for pair in PAIRS * 2]
+    outs += [((main, stream[2] * TILE), BF16) for stream in STREAMS * 2]
     return pl.pallas_call(
         main_kernel,
         in_specs=[pl.BlockSpec(memory_space=pltpu.SMEM)] + [vmem] * 3,
         out_specs=[vmem] * len(outs),
         out_shape=[jax.ShapeDtypeStruct(s, d) for s, d in outs],
         scratch_shapes=[pltpu.VMEM(square, BF16)]
-        + [pltpu.VMEM((main, tokens), BF16)] * 4
+        + [pltpu.VMEM((n, tokens), BF16) for n in (main, main // 2) * 2]
         + [
             pltpu.VMEM(square, BF16),
             pltpu.VMEM((tokens, 3 * width), BF16),
@@ -272,92 +289,104 @@
     )(xs, cs, stats, dqkv, qkv_weight)
 
 
-def join_kernel(grad, *refs):
+def join_kernel(bits, *refs):
+    count = len(STREAMS)
+    kept, came, kept_on, sent_on = (refs[i * count : (i + 1) * count] for i in range(4))
+    half = TILE // 2
+    for i, (_, (_, bit), blocks) in enumerate(STREAMS):
+        for c in range(blocks):
+            at = c * TILE
+            both = kept[i][:, at : at + TILE].astype(F32) + came[i][:, at : at + TILE].astype(F32)
+            low, high = both[:, :half], both[:, half:]
+            same = is_own(lax.broadcasted_iota(jnp.int32, low.shape, 0), bits, bit)
+            kept_on[i][:, c * half : (c + 1) * half] = jnp.where(same, low, high).astype(BF16)
+            sent_on[i][:, c * half : (c + 1) * half] = jnp.where(same, high, low).astype(BF16)
+
+
+def join(bits, pairs):
+    vmem = pl.BlockSpec(memory_space=pltpu.VMEM)
+    shapes = [(a.shape[0], a.shape[1] // 2) for a in pairs]
+    return pl.pallas_call(
+        join_kernel,
+        in_specs=[pl.BlockSpec(memory_space=pltpu.SMEM)] + [vmem] * len(pairs),
+        out_specs=[vmem] * len(pairs),
+        out_shape=[jax.ShapeDtypeStruct(s, BF16) for s in shapes],
+        name="join",
+        **parameters(16, 0, 8 * 10**6),
+    )(bits, *pairs)
+
+
+def join_last_kernel(grad, *refs):
     *pairs, out = refs
     at = grad.shape[1]
     out[:, :at] = grad[...]
-    for keep, came in zip(pairs[: len(PAIRS)], pairs[len(PAIRS) :], strict=True):
+    for keep, came in zip(pairs[: len(STREAMS)], pairs[len(STREAMS) :], strict=True):
         count = keep.shape[1]
         out[:, at : at + count] = (keep[...].astype(F32) + came[...].astype(F32)).astype(BF16)
         at += count
 
 
-def join(grad, pairs):
-    rows = grad.shape[0]
-    arrays = [grad, *pairs]
+def join_last(grad, pairs):
+    vmem = pl.BlockSpec(memory_space=pltpu.VMEM)
     width = grad.shape[1] + sum(a.shape[1] for a in pairs) // 2
-    block = lambda count: pl.BlockSpec((rows // 4, count), lambda i: (i, 0))
-    return pl.pallas_call(
-        join_kernel,
-        grid=(4,),
-        in_specs=[block(a.shape[1]) for a in arrays],
-        out_specs=block(width),
-        out_shape=jax.ShapeDtypeStruct((rows, width), BF16),
-        name="join",
-        **parameters(16, 0, 8 * 10**6),
-    )(*arrays)
+    return pl.pallas_call(
+        join_last_kernel,
+        in_specs=[vmem] * (1 + len(pairs)),
+        out_specs=vmem,
+        out_shape=jax.ShapeDtypeStruct((grad.shape[0], width), BF16),
+        name="join_last",
+        **parameters(16, 0, 4 * 10**6),
+    )(grad, *pairs)
 
 
 def finish_kernel(bits, got, grad, qkv_grad, out_grad, total):
-    step = pl.program_id(0)
-    rows = got.shape[0]
-    width = grad.shape[1]
-    half = width // 2
-    packed = width + half
-    main = 8 * grad.shape[0] // 12
-    grad[pl.ds(pl.multiple_of(step * rows, 16), rows), :] = got[:, :width]
-    pick = one_hot((rows // 2, rows), lambda k: (k // 4) * 8 + k % 4)
-    pick_low = one_hot((rows // 2, rows), lambda k: (k // 4) * 8 + 4 + k % 4)
-    tail = pl.ds(pl.multiple_of(main + step * (rows // 2), 16), rows // 2)
-    grad[tail, :half] = nn(pick, got[:, width:packed]).astype(BF16)
-    grad[tail, half:] = nn(pick_low, got[:, width:packed]).astype(BF16)
-
-    @pl.when(step == 0)
-    def _():
-        total[...] = jnp.zeros_like(total)
-
+    rows, width = got.shape[0], out_grad.shape[1]
+    packed = width + width // 2
+    grad[:rows, :] = got[:, :width]
+    part = 128
+    pick = one_hot((part // 2, part), lambda k: (k // 4) * 8 + k % 4)
+    pick_low = one_hot((part // 2, part), lambda k: (k // 4) * 8 + 4 + k % 4)
+    for i in range(0, rows, part):
+        tail = slice(rows + i // 2, rows + (i + part) // 2)
+        grad[tail, : width // 2] = nn(pick, got[i : i + part, width:packed]).astype(BF16)
+        grad[tail, width // 2 :] = nn(pick_low, got[i : i + part, width:packed]).astype(BF16)
+    peers = got.shape[0] // 8
+    half = TILE // 2
     blocks = width // TILE
-    places = [i for i, pair in enumerate(PAIRS) for _ in range(pair[3])]
-    for block, direction in enumerate(places):
-        first = packed + block * TILE
-        came = got[:, first : first + TILE].astype(F32)
-        bit = PAIRS[direction][2]
-        if rows <= 8 << bit:
-            every = came.reshape(-1, 8, TILE).sum(axis=0)
-            odd = (step * rows // (8 << bit)) % 2 == 1
-            low, high = jnp.where(odd, 0.0, every), jnp.where(odd, every, 0.0)
-        else:
-            runs = came.reshape(-1, 8 << bit, TILE)
-            low = sum(runs[i].reshape(-1, 8, TILE).sum(axis=0) for i in range(0, runs.shape[0], 2))
-            high = sum(runs[i].reshape(-1, 8, TILE).sum(axis=0) for i in range(1, runs.shape[0], 2))
+    places = [stream for stream in STREAMS for _ in range(stream[2])]
+    for block, ((_, first), (_, second), _) in enumerate(places):
+        at = packed + block * half
+        came = got[:, at : at + half].astype(F32)
+        sums = {}
+        for s in range(peers):
+            key = (s >> first) & 1, (s >> second) & 1
+            more = came[8 * s : 8 * s + 8]
+            sums[key] = sums[key] + more if key in sums else more
         at = (2 * (block // blocks) * blocks + block % blocks) * TILE
-        total[:, at : at + TILE] += jnp.where(bits[direction] == 0, low, high)
-        total[:, at + width : at + width + TILE] += jnp.where(bits[direction] == 0, high, low)
-
-    @pl.when(step == pl.num_programs(0) - 1)
-    def _():
-        q, k, v, o, low, high = (total[:, i * width : (i + 1) * width] for i in range(6))
-        for part, (top, end) in enumerate(((q, low[:4]), (k, high[:4]), (v, low[4:]))):
-            qkv_grad[:8, part * width : (part + 1) * width] = top
-            qkv_grad[8:12, part * width : (part + 1) * width] = end
-        out_grad[:8, :] = o
-        out_grad[8:12, :] = high[4:]
+        for i in range(2):
+            for j in range(2):
+                mine = [jnp.where(bits[second] == j, sums[a, 0], sums[a, 1]) for a in range(2)]
+                to = at + i * width + j * half
+                total[:, to : to + half] = jnp.where(bits[first] == i, mine[0], mine[1])
+    q, k, v, o, low, high = (total[:, i * width : (i + 1) * width] for i in range(6))
+    for part, (top, end) in enumerate(((q, low[:4]), (k, high[:4]), (v, low[4:]))):
+        qkv_grad[:8, part * width : (part + 1) * width] = top
+        qkv_grad[8:12, part * width : (part + 1) * width] = end
+    out_grad[:8, :] = o
+    out_grad[8:12, :] = high[4:]
 
 
 def finish(bits, got, tokens, width):
-    steps = 4
-    rows = got.shape[0] // steps
-    whole = lambda shape: pl.BlockSpec(shape, lambda i: (0, 0))
-    shapes = ((tokens, width), (12, 3 * width), (12, width))
+    vmem = pl.BlockSpec(memory_space=pltpu.VMEM)
     return pl.pallas_call(
         finish_kernel,
-        grid=(steps,),
-        in_specs=[pl.BlockSpec(memory_space=pltpu.SMEM), pl.BlockSpec((rows, got.shape[1]), lambda i: (i, 0))],
-        out_specs=[whole(s) for s in shapes],
-        out_shape=[jax.ShapeDtypeStruct(s, d) for s, d in zip(shapes, (BF16, F32, F32), strict=True)],
+        in_specs=[pl.BlockSpec(memory_space=pltpu.SMEM), vmem],
+        out_specs=[vmem] * 3,
+        out_shape=[jax.ShapeDtypeStruct((tokens, width), BF16)]
+        + [jax.ShapeDtypeStruct((12, n), F32) for n in (3 * width, width)],
         scratch_shapes=[pltpu.VMEM((8, 6 * width), F32)],
         name="finish",
-        **parameters(24, 10**9, 5 * 10**6),
+        **parameters(16, 10**7, 2 * 10**6),
     )(bits, got)
 
 
@@ -371,16 +400,23 @@
     )
     row, col = lax.axis_index("row"), lax.axis_index("col")
     place = row * grid_cols + col
-    bits = jnp.stack([place // (1 << bit) % 2 for _, _, bit, _ in PAIRS]).astype(jnp.int32)
+    bits = jnp.stack([place // (1 << bit) % 2 for bit in range(6)]).astype(jnp.int32)
     sent = pack_tokens(activations.reshape(tokens, width), cotangent.reshape(tokens, width), peers)
     sent, bits = lax.optimization_barrier((sent, bits))
     xs, cs, stats, dqkv, *pairs = main_part(bits, exchange(sent), qkv_weight, out_weight, tokens)
-    came = [
-        lax.ppermute(x, axis, [(i, i ^ other) for i in range(lax.axis_size(axis))])
-        for x, (axis, other, _, _) in zip(pairs[len(PAIRS) :], PAIRS, strict=True)
-    ]
+    count = len(STREAMS)
+
+    def swap(arrays, level):
+        return [
+            lax.ppermute(x, ("row", "col"), [(i, i ^ stream[level][0]) for i in range(peers)])
+            for x, stream in zip(arrays, STREAMS, strict=True)
+        ]
+
+    came = swap(pairs[count:], 0)
     grads = token_part(xs, cs, stats, dqkv, qkv_weight, peers * 8)
-    got = exchange(join(grads, (*pairs[: len(PAIRS)], *came)))
+    grads, *came = lax.optimization_barrier((grads, *came))
+    pairs = join(bits, (*pairs[:count], *came))
+    got = exchange(join_last(grads, (*pairs[:count], *swap(pairs[count:], 1))))
     input_grad, qkv_weight_grad, out_weight_grad = finish(bits, got, tokens, width)
     return (input_grad.reshape(rows_dev, cols_dev, width), qkv_weight_grad, out_weight_grad)
 

time: 139 us -> 135 us (0.971)
  blocking collectives: 93.2 us -> 79.4 us
  waiting for transfers between devices: 3.94 us -> 9.37 us
  starting transfers between devices: 3.48 us -> 8.51 us
    all_to_all x1, blocking collectives: 48.6 us -> 34.9 us  [local(): got = exchange(join_last(grads, (*pairs[:count], *swap(pairs[count:], 1))))]
    ppermute x5 -> x10, waiting for transfers between devices: 3.94 us -> 9.37 us  [swap(): lax.ppermute(x, ('row', 'col'), [(i, i ^ stream[level][0]) for i in range...]
    ppermute x5 -> x10, starting transfers between devices: 3.48 us -> 8.51 us  [swap(): lax.ppermute(x, ('row', 'col'), [(i, i ^ stream[level][0]) for i in range...]
    pallas_call x1, Pallas kernels: 23.4 us -> 21.6 us  [main_part(): pl.pallas_call(main_kernel, in_specs=[pl.BlockSpec(memory_space=pltpu.SME...]
    pallas_call x2 -> x3, Pallas kernels: 3.44 us -> 4.16 us  [the longest x1 2 us: finish(): pl.pallas_call(finish_kernel, in_specs=[pl.BlockSpec(memory_space=pltpu.S...]
  transfers between devices with their start and end apart: 5 -> 10, of which waited for: 4 -> 5; matrix products, arithmetic and copies ran while one was open for 0% -> 0% of each run, Pallas kernels for 5% -> 5%
where the time goes in v4:
time: 135 us
  blocking collectives  79.4 us (59%)
  Pallas kernels  34 us (25%)
  waiting for transfers between devices  9.37 us (7%)
  starting transfers between devices  8.51 us (6%)
  local copies, waits for them, and re-layouts  2.63 us (2%)
    all_to_all x1, blocking collectives, local(): exchange(sent)  44.5 us
    all_to_all x1, blocking collectives, local(): got = exchange(join_last(grads, (*pairs[:count], *swap(pairs[count:], 1))))  34.9 us
    pallas_call x1, Pallas kernels, main_part(): pl.pallas_call(main_kernel, in_specs=[pl.BlockSpec(memory_space=pltpu.SME...  21.6 us
    ppermute x10, waiting for transfers between devices, swap(): lax.ppermute(x, ('row', 'col'), [(i, i ^ stream[level][0]) for i in range...  9.37 us
    ppermute x10, starting transfers between devices, swap(): lax.ppermute(x, ('row', 'col'), [(i, i ^ stream[level][0]) for i in range...  8.51 us
    pallas_call x1, Pallas kernels, token_part(): pl.pallas_call(token_kernel, in_specs=[vmem] * 5, out_specs=vmem, out_sha...  7.18 us
  transfers between devices with their start and end apart: 10, of which 5 were waited for; matrix products, arithmetic and copies ran while one was open for 0% of the time, Pallas kernels for 5%

profile of v4, /device:TPU:0, one launch (start us, length us, event | category | flops | bytes accessed | tf_op | source)
XLA Modules:
  0.0 134.7 jit_solution(17818885769066912111)
XLA Ops:
  0.8 0.0 copy-start
  0.8 1.3 copy-done
  2.0 1.3 copy-done.1
  3.3 1.0 pack_tokens.1
  4.3 0.1 stack.27.bits
  4.4 44.5 %all_to_all.22 = bf16[64,8,2304]{2,1,0:T(8,128)(2,1)S(1)} all-to-all(bf16[64,8,2304]{2,1,0:T(8,128)(2,1)S(1)} %bitcast.13), channel_id=1, replica_groups=mesh['scene'=2,'row'=8,'col'=8] {'row','col'}, dimensions={0} | all-to-all | bytes 4718592 | tf_op jit(solution)/shard_map/all_to_all | solution.py:406
  49.0 21.6 %main_part.1 = (bf16[768,768]{1,0:T(8,128)(2,1)S(1)}, bf16[768,768]{1,0:T(8,128)(2,1)S(1)}, f32[768,256]{1,0:T(8,128)S(1)}, bf16[768,2304]{1,0:T(8,128)(2,1)S(1)...) custom-call(s32[6]{0:T(128)S(1)} %stack.27.bits, ...), custom_call_target="tpu_custom_call" | custom-call | flops 16000000000 | bytes 30000000 | tf_op jit(solution)/shard_map/main_part/pallas_call | solution.py:235
  70.6 0.9 collective-permute-start
  71.5 1.2 collective-permute-start.1
  72.7 0.7 collective-permute-start.2
  73.4 0.5 collective-permute-start.3
  73.9 0.3 collective-permute-start.4
  74.2 7.2 %token_grad.1.grad = bf16[512,1152]{1,0:T(8,128)(2,1)S(1)} custom-call(bf16[768,768]{1,0:T(8,128)(2,1)S(1)} %get-tuple-element.40.xs, bf16[768,768]{1,0:T(8,128)(2,1)S(1)} %get-tuple-element.41.cs, f32[768,256]{1,0:T(8,128)S(1)} %get-tuple-element.42.stats, bf16[768,2304]{1,0:T(8,128)(2,1)S(1)} %get-tuple-element.43.dqkv, bf16[768,2304]{1,0:T(8,128)(2,1)S(1)} %copy-done.2), custom_call_target="tpu_custom_call" | custom-call | flops 4000000000 | bytes 12000000 | tf_op jit(solution)/shard_map/token_grad/pallas_call | solution.py:281
  81.4 0.1 collective-permute-done.4.refs_9_
  81.5 1.5 %collective-permute-done.refs_5_ = bf16[512,512]{1,0:T(8,128)(2,1)S(1)} collective-permute-done((bf16[512,512]{1,0:T(8,128)(2,1)S(1)}, bf16[512,512]{1,0:T(8,128)(2,1)S(1)}, u32[]{:S(2)}, u32[]{:S(2)}) %collective-permute-start) | collective-permute-done | bytes 524320 | tf_op jit(solution)/shard_map/ppermute | solution.py:411
  83.0 1.7 %collective-permute-done.1.refs_6_ = bf16[512,512]{1,0:T(8,128)(2,1)S(1)} collective-permute-done((bf16[512,512]{1,0:T(8,128)(2,1)S(1)}, bf16[512,512]{1,0:T(8,128)(2,1)S(1)}, u32[]{:S(2)}, u32[]{:S(2)}) %collective-permute-start.1) | collective-permute-done | bytes 524320 | tf_op jit(solution)/shard_map/ppermute | solution.py:411
  84.7 0.0 collective-permute-done.2.refs_7_
  84.7 0.7 collective-permute-done.3.refs_8_
  85.4 1.8 %join.1 = (bf16[512,256]{1,0:T(8,128)(2,1)S(1)}, bf16[512,256]{1,0:T(8,128)(2,1)S(1)}, bf16[512,256]{1,0:T(8,128)(2,1)S(1)}, bf16[512,256]{1,0:T(8,128)(2,1)S(1)...) custom-call(s32[6]{0:T(128)S(1)} %stack.27.bits, ...), custom_call_target="tpu_custom_call" | custom-call | bytes 8000000 | tf_op jit(solution)/shard_map/join/pallas_call | solution.py:309
  87.2 0.9 collective-permute-start.5
  88.1 0.9 collective-permute-start.6
  89.0 0.7 collective-permute-start.7
  89.7 1.6 %collective-permute-start.8 = (bf16[512,256]{1,0:T(8,128)(2,1)S(1)}, bf16[512,256]{1,0:T(8,128)(2,1)S(1)}, u32[]{:S(2)}, u32[]{:S(2)}) collective-permute-start(bf16[512,256]{1,0:T(8,128)(2,1)S(1)} %get-tuple-element.68), channel_id=1, source_target_pairs={{0,48},{1,49},{2,50},{3,51},{4,52},{5,53},{6,54},{7,55},{8,56},{9,... | collective-permute-start | bytes 786440 | tf_op jit(solution)/shard_map/ppermute | solution.py:411
  91.3 0.8 collective-permute-start.9
  92.1 5.4 %collective-permute-done.9.refs_9_ = bf16[512,128]{1,0:T(8,128)(2,1)S(1)} collective-permute-done((bf16[512,128]{1,0:T(8,128)(2,1)S(1)}, bf16[512,128]{1,0:T(8,128)(2,1)S(1)}, u32[]{:S(2)}, u32[]{:S(2)}) %collective-permute-start.9) | collective-permute-done | bytes 131104 | tf_op jit(solution)/shard_map/ppermute | solution.py:411
  97.5 0.0 collective-permute-done.5.refs_5_
  97.5 0.0 collective-permute-done.6.refs_6_
  97.5 0.0 collective-permute-done.7.refs_7_
  97.5 0.0 collective-permute-done.8.refs_8_
  97.5 0.4 join_last.1
  97.9 34.9 %all_to_all.23 = bf16[64,8,2304]{2,1,0:T(8,128)(2,1)S(1)} all-to-all(bf16[64,8,2304]{2,1,0:T(8,128)(2,1)S(1)} %bitcast.15), channel_id=1, replica_groups=mesh['scene'=2,'row'=8,'col'=8] {'row','col'}, dimensions={0} | all-to-all | bytes 4718592 | tf_op jit(solution)/shard_map/all_to_all | solution.py:419
  132.7 2.0 %finish.1 = (bf16[768,768]{1,0:T(8,128)(2,1)}, f32[12,2304]{1,0:T(8,128)}, f32[12,768]{1,0:T(8,128)}) custom-call(s32[6]{0:T(128)S(1)} %stack.27.bits, bf16[512,2304]{1,0:T(8,128)(2,1)S(1)} %bitcast.14), custom_call_target="tpu_custom_call" | custom-call | flops 10000000 | bytes 2000000 | tf_op jit(solution)/shard_map/finish/pallas_call | solution.py:381
  (5 shorter events, 0.0 us)
Async XLA Ops:
  0.8 1.3 copy-start
  2.0 1.3 copy-start.1
  4.4 44.6 %copy-start.2 = (bf16[768,2304]{1,0:T(8,128)(2,1)S(1)}, bf16[768,2304]{1,0:T(8,128)(2,1)}, u32[]{:S(2)}) copy-start(bf16[768,2304]{1,0:T(8,128)(2,1)} %qkv_w.3) | copy-start | bytes 10616836
  4.4 44.6 %copy-start.3 = (bf16[768,768]{1,0:T(8,128)(2,1)S(1)}, bf16[768,768]{1,0:T(8,128)(2,1)}, u32[]{:S(2)}) copy-start(bf16[768,768]{1,0:T(8,128)(2,1)} %out_w.1) | copy-start | bytes 3538948
  70.6 12.4 %collective-permute-start = (bf16[512,512]{1,0:T(8,128)(2,1)S(1)}, bf16[512,512]{1,0:T(8,128)(2,1)S(1)}, u32[]{:S(2)}, u32[]{:S(2)}) collective-permute-start(bf16[512,512]{1,0:T(8,128)(2,1)S(1)} %get-tuple-element.44), channel_id=1, source_target_pairs={{0,16},{1,17},{2,18},{3,19},{4,20},{5,21},{6,22},{7,23},{8,24},{9,... | collective-permute-start | bytes 1572872 | tf_op jit(solution)/shard_map/ppermute | solution.py:411
  71.5 13.2 %collective-permute-start.1 = (bf16[512,512]{1,0:T(8,128)(2,1)S(1)}, bf16[512,512]{1,0:T(8,128)(2,1)S(1)}, u32[]{:S(2)}, u32[]{:S(2)}) collective-permute-start(bf16[512,512]{1,0:T(8,128)(2,1)S(1)} %get-tuple-element.45), channel_id=1, source_target_pairs={{0,48},{1,49},{2,50},{3,51},{4,52},{5,53},{6,54},{7,55},{8,56},{9,... | collective-permute-start | bytes 1572872 | tf_op jit(solution)/shard_map/ppermute | solution.py:411
  72.7 12.0 %collective-permute-start.2 = (bf16[512,512]{1,0:T(8,128)(2,1)S(1)}, bf16[512,512]{1,0:T(8,128)(2,1)S(1)}, u32[]{:S(2)}, u32[]{:S(2)}) collective-permute-start(bf16[512,512]{1,0:T(8,128)(2,1)S(1)} %get-tuple-element.46), channel_id=1, source_target_pairs={{0,8},{1,9},{2,10},{3,11},{4,12},{5,13},{6,14},{7,15},{8,0},{9,1},... | collective-permute-start | bytes 1572872 | tf_op jit(solution)/shard_map/ppermute | solution.py:411
  73.4 12.0 %collective-permute-start.3 = (bf16[512,512]{1,0:T(8,128)(2,1)S(1)}, bf16[512,512]{1,0:T(8,128)(2,1)S(1)}, u32[]{:S(2)}, u32[]{:S(2)}) collective-permute-start(bf16[512,512]{1,0:T(8,128)(2,1)S(1)} %get-tuple-element.47), channel_id=1, source_target_pairs={{0,2},{1,3},{2,0},{3,1},{4,6},{5,7},{6,4},{7,5},{8,10},{9,11},{10,... | collective-permute-start | bytes 1572872 | tf_op jit(solution)/shard_map/ppermute | solution.py:411
  73.9 7.6 %collective-permute-start.4 = (bf16[512,256]{1,0:T(8,128)(2,1)S(1)}, bf16[512,256]{1,0:T(8,128)(2,1)S(1)}, u32[]{:S(2)}, u32[]{:S(2)}) collective-permute-start(bf16[512,256]{1,0:T(8,128)(2,1)S(1)} %get-tuple-element.48), channel_id=1, source_target_pairs={{0,6},{1,7},{2,4},{3,5},{4,2},{5,3},{6,0},{7,1},{8,14},{9,15},{10,... | collective-permute-start | bytes 786440 | tf_op jit(solution)/shard_map/ppermute | solution.py:411
  87.2 10.3 %collective-permute-start.5 = (bf16[512,256]{1,0:T(8,128)(2,1)S(1)}, bf16[512,256]{1,0:T(8,128)(2,1)S(1)}, u32[]{:S(2)}, u32[]{:S(2)}) collective-permute-start(bf16[512,256]{1,0:T(8,128)(2,1)S(1)} %get-tuple-element.65), channel_id=1, source_target_pairs={{0,8},{1,9},{2,10},{3,11},{4,12},{5,13},{6,14},{7,15},{8,0},{9,1},... | collective-permute-start | bytes 786440 | tf_op jit(solution)/shard_map/ppermute | solution.py:411
  88.1 9.4 %collective-permute-start.6 = (bf16[512,256]{1,0:T(8,128)(2,1)S(1)}, bf16[512,256]{1,0:T(8,128)(2,1)S(1)}, u32[]{:S(2)}, u32[]{:S(2)}) collective-permute-start(bf16[512,256]{1,0:T(8,128)(2,1)S(1)} %get-tuple-element.66), channel_id=1, source_target_pairs={{0,2},{1,3},{2,0},{3,1},{4,6},{5,7},{6,4},{7,5},{8,10},{9,11},{10,... | collective-permute-start | bytes 786440 | tf_op jit(solution)/shard_map/ppermute | solution.py:411
  89.0 8.5 %collective-permute-start.7 = (bf16[512,256]{1,0:T(8,128)(2,1)S(1)}, bf16[512,256]{1,0:T(8,128)(2,1)S(1)}, u32[]{:S(2)}, u32[]{:S(2)}) collective-permute-start(bf16[512,256]{1,0:T(8,128)(2,1)S(1)} %get-tuple-element.67), channel_id=1, source_target_pairs={{0,16},{1,17},{2,18},{3,19},{4,20},{5,21},{6,22},{7,23},{8,24},{9,... | collective-permute-start | bytes 786440 | tf_op jit(solution)/shard_map/ppermute | solution.py:411
  89.7 7.8 %collective-permute-start.8 = (bf16[512,256]{1,0:T(8,128)(2,1)S(1)}, bf16[512,256]{1,0:T(8,128)(2,1)S(1)}, u32[]{:S(2)}, u32[]{:S(2)}) collective-permute-start(bf16[512,256]{1,0:T(8,128)(2,1)S(1)} %get-tuple-element.68), channel_id=1, source_target_pairs={{0,48},{1,49},{2,50},{3,51},{4,52},{5,53},{6,54},{7,55},{8,56},{9,... | collective-permute-start | bytes 786440 | tf_op jit(solution)/shard_map/ppermute | solution.py:411
  91.3 6.2 %collective-permute-start.9 = (bf16[512,128]{1,0:T(8,128)(2,1)S(1)}, bf16[512,128]{1,0:T(8,128)(2,1)S(1)}, u32[]{:S(2)}, u32[]{:S(2)}) collective-permute-start(bf16[512,128]{1,0:T(8,128)(2,1)S(1)} %get-tuple-element.69), channel_id=1, source_target_pairs={{0,9},{1,8},{2,11},{3,10},{4,13},{5,12},{6,15},{7,14},{8,1},{9,0},... | collective-permute-start | bytes 393224 | tf_op jit(solution)/shard_map/ppermute | solution.py:411

commit v5 on v4

--- a/solution.py
+++ b/solution.py
@@ -16,13 +16,10 @@
 
 SEQ = 64
 LANES = 128
-STREAMS = (
-    ((16, 4), (8, 3), 2),
-    ((48, 5), (2, 1), 2),
-    ((8, 3), (16, 4), 2),
-    ((2, 1), (48, 5), 2),
-    ((6, 2), (9, 0), 1),
-)
+LOG2_E = 1.4426950408889634
+FIRST = (((16, 4), (8, 3), 2), ((48, 5), (2, 1), 2), ((8, 3), (16, 4), 2))
+LAST = (((2, 1), (48, 5), 2), ((6, 2), (9, 0), 1))
+STREAMS = FIRST + LAST
 TILE = 256
 
 
@@ -132,7 +129,7 @@
         probs_low, score_low = [], []
         for score, prob_grad in zip(scores, prob_grads):
             top = jnp.max(score, axis=0, keepdims=True)
-            e = jnp.exp((score - top) * scaling)
+            e = jnp.exp2((score - top) * (scaling * LOG2_E))
             probs = e * (1.0 / jnp.sum(e, axis=0, keepdims=True))
             delta = jnp.sum(probs * prob_grad, axis=0, keepdims=True)
             probs_low.append(probs.astype(BF16))
@@ -159,9 +156,8 @@
 def main_kernel(
     bits, got, qkv_w, out_w, xs, cs, stats, dqkv, *refs
 ):
-    count = len(STREAMS)
-    kept, sent = refs[:count], refs[count : 2 * count]
-    ns, nt1, nt2, at1, at2, att, qkv, og, order = refs[2 * count :]
+    ns, att, *pairs = refs[: 2 + 2 * len(FIRST)]
+    nt1, at1, qkv, og, order = refs[2 + 2 * len(FIRST) :]
     width = out_w.shape[0]
     half = width // 2
     tokens = xs.shape[0]
@@ -177,7 +173,7 @@
         to[main:, :half] = tail[:rest]
         to[main:, half:] = tail[rest:]
 
-    @pl.loop(0, tokens // SEQ, unroll=4)
+    @pl.loop(0, tokens // SEQ, unroll=12)
     def _(g):
         rows = rows_of(g)
         x = xs[rows, :].astype(F32)
@@ -191,38 +187,31 @@
     project(ns, cs, qkv_w, out_w, qkv, og)
     attend(qkv, og, dqkv, att, 2)
 
-    eight, four = eight_rows((main, width)), four_rows((main // 2, width))
-    for pick, source, to in ((eight, ns, nt1), (four, ns, nt2), (eight, att, at1), (four, att, at2)):
-        to[...] = nt(pick, source[...]).astype(BF16)
-    tile = TILE
-    shape = (main, tile)
-    place = lax.broadcasted_iota(jnp.int32, shape, 0)
-    is_upper = lax.broadcasted_iota(jnp.int32, (main // 16, 8, tile), 1) < 4
-
-    def under(a, b):
-        a, b = a.reshape(is_upper.shape), b.reshape(is_upper.shape)
-        first = jnp.where(is_upper, a, pltpu.roll(b, 4, 1))
-        second = jnp.where(is_upper, pltpu.roll(a, 4, 1), b)
-        return jnp.stack([first, second], axis=1).reshape(shape)
-
-    def share(keep, send, c, low, high, direction):
-        same = is_own(place, bits, STREAMS[direction][0][1])
-        keep[:, c : c + tile] = jnp.where(same, low, high).astype(BF16)
-        send[:, c : c + tile] = jnp.where(same, high, low).astype(BF16)
-
-    places = [(i, c) for i, pair in enumerate(STREAMS) for c in range(0, pair[2] * tile, tile)]
-    for c in range(0, width, tile):
-        q, k, v = (slice(part * width + c, part * width + c + tile) for part in range(3))
-        for kind in range(3):
+    eight = eight_rows((main, width))
+    nt1[...] = nt(eight, ns[...]).astype(BF16)
+    at1[...] = nt(eight, att[...]).astype(BF16)
+    targets = places(pairs, FIRST)
+    for kind in range(2):
+        for c in range(0, width, TILE):
+            q, k, v = (slice(part * width + c, part * width + c + TILE) for part in range(3))
             if kind == 0:
                 low, high = nn(nt1[...], dqkv[:, q]), nn(nt1[...], dqkv[:, k])
-            elif kind == 1:
+            else:
                 low, high = nn(nt1[...], dqkv[:, v]), nn(at1[...], cs[:, q])
-            else:
-                low = under(nn(nt2[...], dqkv[:, q]), nn(nt2[...], dqkv[:, v]))
-                high = under(nn(nt2[...], dqkv[:, k]), nn(at2[...], cs[:, q]))
-            direction, to = places[kind * (width // tile) + c // tile]
-            share(kept[direction], sent[direction], to, low, high, direction)
+            share(bits, next(targets), low, high)
+
+
+def places(pairs, streams):
+    for i, stream in enumerate(streams):
+        for c in range(0, stream[2] * TILE, TILE):
+            yield stream, pairs[i], pairs[len(streams) + i], c
+
+
+def share(bits, target, low, high):
+    ((_, bit), *_), keep, send, c = target
+    same = is_own(lax.broadcasted_iota(jnp.int32, low.shape, 0), bits, bit)
+    keep[:, c : c + TILE] = jnp.where(same, low, high).astype(BF16)
+    send[:, c : c + TILE] = jnp.where(same, high, low).astype(BF16)
 
 
 def main_part(bits, got, qkv_weight, out_weight, tokens):
@@ -231,16 +220,16 @@
     vmem = pl.BlockSpec(memory_space=pltpu.VMEM)
     square = (tokens, width)
     outs = [(square, BF16), (square, BF16), ((tokens, 2 * LANES), F32), ((tokens, 3 * width), BF16)]
-    outs += [((main, stream[2] * TILE), BF16) for stream in STREAMS * 2]
+    outs += [(square, BF16), (square, BF16)]
+    outs += [((main, stream[2] * TILE), BF16) for stream in FIRST * 2]
     return pl.pallas_call(
         main_kernel,
         in_specs=[pl.BlockSpec(memory_space=pltpu.SMEM)] + [vmem] * 3,
         out_specs=[vmem] * len(outs),
         out_shape=[jax.ShapeDtypeStruct(s, d) for s, d in outs],
-        scratch_shapes=[pltpu.VMEM(square, BF16)]
-        + [pltpu.VMEM((n, tokens), BF16) for n in (main, main // 2) * 2]
-        + [
-            pltpu.VMEM(square, BF16),
+        scratch_shapes=[
+            pltpu.VMEM((main, tokens), BF16),
+            pltpu.VMEM((main, tokens), BF16),
             pltpu.VMEM((tokens, 3 * width), BF16),
             pltpu.VMEM(square, BF16),
             pltpu.VMEM((main, main), BF16),
@@ -250,6 +239,44 @@
     )(bits, got, qkv_weight, out_weight)
 
 
+def rest_kernel(bits, cs, dqkv, ns, att, *refs):
+    *pairs, nt2, at2 = refs
+    tokens, width = cs.shape
+    main = 2 * nt2.shape[0]
+    four = four_rows((main // 2, width))
+    nt2[...] = nt(four, ns[...]).astype(BF16)
+    at2[...] = nt(four, att[...]).astype(BF16)
+    is_upper = lax.broadcasted_iota(jnp.int32, (main // 16, 8, TILE), 1) < 4
+
+    def under(a, b):
+        a, b = a.reshape(is_upper.shape), b.reshape(is_upper.shape)
+        first = jnp.where(is_upper, a, pltpu.roll(b, 4, 1))
+        second = jnp.where(is_upper, pltpu.roll(a, 4, 1), b)
+        return jnp.stack([first, second], axis=1).reshape(main, TILE)
+
+    targets = places(pairs, LAST)
+    for c in range(0, width, TILE):
+        q, k, v = (slice(part * width + c, part * width + c + TILE) for part in range(3))
+        low = under(nn(nt2[...], dqkv[:, q]), nn(nt2[...], dqkv[:, v]))
+        high = under(nn(nt2[...], dqkv[:, k]), nn(at2[...], cs[:, q]))
+        share(bits, next(targets), low, high)
+
+
+def rest_part(bits, cs, dqkv, ns, att, main):
+    tokens = cs.shape[0]
+    vmem = pl.BlockSpec(memory_space=pltpu.VMEM)
+    shapes = [(main, stream[2] * TILE) for stream in LAST * 2]
+    return pl.pallas_call(
+        rest_kernel,
+        in_specs=[pl.BlockSpec(memory_space=pltpu.SMEM)] + [vmem] * 4,
+        out_specs=[vmem] * len(shapes),
+        out_shape=[jax.ShapeDtypeStruct(s, BF16) for s in shapes],
+        scratch_shapes=[pltpu.VMEM((main // 2, tokens), BF16)] * 2,
+        name="rest_part",
+        **parameters(24, 10**6, 10**5),
+    )(bits, cs, dqkv, ns, att)
+
+
 def token_kernel(xs, cs, stats, dqkv, qkv_w, out, ngs, igs):
     tokens, width = xs.shape
     main = out.shape[0]
@@ -258,7 +285,7 @@
     for f in range(0, width, 256):
         ngs[:, f : f + 256] = nt(dqkv[...], qkv_w[f : f + 256, :])
 
-    @pl.loop(0, tokens // SEQ, unroll=4)
+    @pl.loop(0, tokens // SEQ, unroll=12)
     def _(g):
         rows = rows_of(g)
         inv = stats[rows, LANES:][:, :1]
@@ -285,15 +312,15 @@
         out_shape=jax.ShapeDtypeStruct((main, width + width // 2), BF16),
         scratch_shapes=[pltpu.VMEM((tokens, width), F32), pltpu.VMEM((tokens, width), BF16)],
         name="token_grad",
-        **parameters(20, 4 * 10**9, 12 * 10**6),
+        **parameters(20, 10**6, 10**5),
     )(xs, cs, stats, dqkv, qkv_weight)
 
 
-def join_kernel(bits, *refs):
-    count = len(STREAMS)
+def join_kernel(streams, bits, *refs):
+    count = len(streams)
     kept, came, kept_on, sent_on = (refs[i * count : (i + 1) * count] for i in range(4))
     half = TILE // 2
-    for i, (_, (_, bit), blocks) in enumerate(STREAMS):
+    for i, (_, (_, bit), blocks) in enumerate(streams):
         for c in range(blocks):
             at = c * TILE
             both = kept[i][:, at : at + TILE].astype(F32) + came[i][:, at : at + TILE].astype(F32)
@@ -303,16 +330,16 @@
             sent_on[i][:, c * half : (c + 1) * half] = jnp.where(same, high, low).astype(BF16)
 
 
-def join(bits, pairs):
+def join(streams, bits, pairs):
     vmem = pl.BlockSpec(memory_space=pltpu.VMEM)
     shapes = [(a.shape[0], a.shape[1] // 2) for a in pairs]
     return pl.pallas_call(
-        join_kernel,
+        functools.partial(join_kernel, streams),
         in_specs=[pl.BlockSpec(memory_space=pltpu.SMEM)] + [vmem] * len(pairs),
         out_specs=[vmem] * len(pairs),
         out_shape=[jax.ShapeDtypeStruct(s, BF16) for s in shapes],
         name="join",
-        **parameters(16, 0, 8 * 10**6),
+        **parameters(16, 10**4, 10**4),
     )(bits, *pairs)
 
 
@@ -403,20 +430,27 @@
     bits = jnp.stack([place // (1 << bit) % 2 for bit in range(6)]).astype(jnp.int32)
     sent = pack_tokens(activations.reshape(tokens, width), cotangent.reshape(tokens, width), peers)
     sent, bits = lax.optimization_barrier((sent, bits))
-    xs, cs, stats, dqkv, *pairs = main_part(bits, exchange(sent), qkv_weight, out_weight, tokens)
-    count = len(STREAMS)
-
-    def swap(arrays, level):
+    xs, cs, stats, dqkv, ns, att, *early = main_part(bits, exchange(sent), qkv_weight, out_weight, tokens)
+
+    def swap(arrays, streams, level):
         return [
             lax.ppermute(x, ("row", "col"), [(i, i ^ stream[level][0]) for i in range(peers)])
-            for x, stream in zip(arrays, STREAMS, strict=True)
+            for x, stream in zip(arrays, streams, strict=True)
         ]
 
-    came = swap(pairs[count:], 0)
+    first, last = len(FIRST), len(LAST)
+    early_came = swap(early[first:], FIRST, 0)
+    late = rest_part(bits, cs, dqkv, ns, att, peers * 8)
+    late_came = swap(late[last:], LAST, 0)
+    dqkv, *_ = lax.optimization_barrier((dqkv, *late))
     grads = token_part(xs, cs, stats, dqkv, qkv_weight, peers * 8)
-    grads, *came = lax.optimization_barrier((grads, *came))
-    pairs = join(bits, (*pairs[:count], *came))
-    got = exchange(join_last(grads, (*pairs[:count], *swap(pairs[count:], 1))))
+    grads, *early_came = lax.optimization_barrier((grads, *early_came))
+    early = join(FIRST, bits, (*early[:first], *early_came))
+    early_came = swap(early[first:], FIRST, 1)
+    grads, *late_came = lax.optimization_barrier((grads, *late_came))
+    late = join(LAST, bits, (*late[:last], *late_came))
+    late_came = swap(late[last:], LAST, 1)
+    got = exchange(join_last(grads, (*early[:first], *late[:last], *early_came, *late_came)))
     input_grad, qkv_weight_grad, out_weight_grad = finish(bits, got, tokens, width)
     return (input_grad.reshape(rows_dev, cols_dev, width), qkv_weight_grad, out_weight_grad)
 

time: 135 us -> 132 us (0.978)
    pallas_call x1 -> x3, Pallas kernels: 1.8 us -> 5.08 us  [the longest x1 2.73 us: rest_part(): pl.pallas_call(rest_kernel, in_specs=[pl.BlockSpec(memory_space=pltpu.SME...]
    pallas_call x1, Pallas kernels: 21.6 us -> 18.7 us  [main_part(): pl.pallas_call(main_kernel, in_specs=[pl.BlockSpec(memory_space=pltpu.SME...]
  transfers between devices with their start and end apart: 10 -> 10, of which waited for: 5 -> 4; matrix products, arithmetic and copies ran while one was open for 0% -> 0% of each run, Pallas kernels for 5% -> 8%
where the time goes in v5:
time: 132 us
  blocking collectives  79.2 us (60%)
  Pallas kernels  33.2 us (25%)
  waiting for transfers between devices  8.51 us (6%)
  starting transfers between devices  7.54 us (6%)
  local copies, waits for them, and re-layouts  2.63 us (2%)
    all_to_all x1, blocking collectives, local(): exchange(sent)  44.5 us
    all_to_all x1, blocking collectives, local(): exchange(join_last(grads, (*early[:first], *late[:last], *early_came, *la...  34.7 us
    pallas_call x1, Pallas kernels, main_part(): pl.pallas_call(main_kernel, in_specs=[pl.BlockSpec(memory_space=pltpu.SME...  18.7 us
    ppermute x10, waiting for transfers between devices, swap(): lax.ppermute(x, ('row', 'col'), [(i, i ^ stream[level][0]) for i in range...  8.51 us
    ppermute x10, starting transfers between devices, swap(): lax.ppermute(x, ('row', 'col'), [(i, i ^ stream[level][0]) for i in range...  7.54 us
    pallas_call x1, Pallas kernels, token_part(): pl.pallas_call(token_kernel, in_specs=[vmem] * 5, out_specs=vmem, out_sha...  6.09 us
    pallas_call x1, Pallas kernels, rest_part(): pl.pallas_call(rest_kernel, in_specs=[pl.BlockSpec(memory_space=pltpu.SME...  2.73 us
  transfers between devices with their start and end apart: 10, of which 4 were waited for; matrix products, arithmetic and copies ran while one was open for 0% of the time, Pallas kernels for 8%

profile of v5, /device:TPU:0, one launch (start us, length us, event | category | flops | bytes accessed | tf_op | source)
XLA Modules:
  0.0 132.0 jit_solution(618986421020066946)
XLA Ops:
  0.8 0.0 copy-start
  0.8 1.3 copy-done
  2.0 1.3 copy-done.1
  3.3 1.0 pack_tokens.1
  4.3 0.1 stack.27.bits
  4.4 44.5 %all_to_all.22 = bf16[64,8,2304]{2,1,0:T(8,128)(2,1)S(1)} all-to-all(bf16[64,8,2304]{2,1,0:T(8,128)(2,1)S(1)} %bitcast.13), channel_id=1, replica_groups=mesh['scene'=2,'row'=8,'col'=8] {'row','col'}, dimensions={0} | all-to-all | bytes 4718592 | tf_op jit(solution)/shard_map/all_to_all | solution.py:433
  49.0 18.7 %main_part.1 = (bf16[768,768]{1,0:T(8,128)(2,1)S(1)}, bf16[768,768]{1,0:T(8,128)(2,1)S(1)}, f32[768,256]{1,0:T(8,128)S(1)}, bf16[768,2304]{1,0:T(8,128)(2,1)S(1)...) custom-call(s32[6]{0:T(128)S(1)} %stack.27.bits, ...), custom_call_target="tpu_custom_call" | custom-call | flops 16000000000 | bytes 30000000 | tf_op jit(solution)/shard_map/main_part/pallas_call | solution.py:225
  67.7 0.7 collective-permute-start
  68.4 1.2 collective-permute-start.1
  69.7 0.7 collective-permute-start.2
  70.3 2.7 %rest_part.1 = (bf16[512,512]{1,0:T(8,128)(2,1)S(1)}, bf16[512,256]{1,0:T(8,128)(2,1)S(1)}, bf16[512,512]{1,0:T(8,128)(2,1)S(1)}, bf16[512,256]{1,0:T(8,128)(2,1)S(1)}) custom-call(s32[6]{0:T(128)S(1)} %stack.27.bits, bf16[768,768]{1,0:T(8,128)(2,1)S(1)} %get-tuple-element.45.cs, bf16[768,2304]{1,0:T(8,128)(2,1)S(1)} %get-tuple-element.54.dqkv, ...), custom_call_target="tpu_custom_call" | custom-call | flops 1000000 | bytes 100000 | tf_op jit(solution)/shard_map/rest_part/pallas_call | solution.py:269
  73.1 0.6 collective-permute-start.3
  73.7 0.3 collective-permute-start.4
  74.0 6.1 %token_grad.1.grad = bf16[512,1152]{1,0:T(8,128)(2,1)S(1)} custom-call(bf16[768,768]{1,0:T(8,128)(2,1)S(1)} %get-tuple-element.44.xs, bf16[768,768]{1,0:T(8,128)(2,1)S(1)} %get-tuple-element.45.cs, f32[768,256]{1,0:T(8,128)S(1)} %get-tuple-element.46.stats, bf16[768,2304]{1,0:T(8,128)(2,1)S(1)} %get-tuple-element.54.dqkv, bf16[768,2304]{1,0:T(8,128)(2,1)S(1)} %copy-done.2), custom_call_target="tpu_custom_call" | custom-call | flops 1000000 | bytes 100000 | tf_op jit(solution)/shard_map/token_grad/pallas_call | solution.py:308
  80.1 0.0 collective-permute-done.refs_3_
  80.1 1.5 %collective-permute-done.1.refs_4_ = bf16[512,512]{1,0:T(8,128)(2,1)S(1)} collective-permute-done((bf16[512,512]{1,0:T(8,128)(2,1)S(1)}, bf16[512,512]{1,0:T(8,128)(2,1)S(1)}, u32[]{:S(2)}, u32[]{:S(2)}) %collective-permute-start.1) | collective-permute-done | bytes 524320 | tf_op jit(solution)/shard_map/ppermute | solution.py:437
  81.6 0.0 collective-permute-done.2.refs_5_
  81.6 1.4 %join.2 = (bf16[512,256]{1,0:T(8,128)(2,1)S(1)}, bf16[512,256]{1,0:T(8,128)(2,1)S(1)}, bf16[512,256]{1,0:T(8,128)(2,1)S(1)}, bf16[512,256]{1,0:T(8,128)(2,1)S(1)...) custom-call(s32[6]{0:T(128)S(1)} %stack.27.bits, bf16[512,512]{1,0:T(8,128)(2,1)S(1)} %get-tuple-element.60.refs_0_, ...), custom_call_target="tpu_custom_call" | custom-call | flops 10000 | bytes 10000 | tf_op jit(solution)/shard_map/join/pallas_call | solution.py:336
  83.0 1.0 collective-permute-start.5
  84.0 0.5 collective-permute-start.6
  84.5 0.5 collective-permute-start.7
  85.0 1.3 collective-permute-done.3.refs_2_
  86.3 1.0 join.3
  87.3 0.9 collective-permute-start.8
  88.2 1.1 collective-permute-start.9
  89.3 5.1 %collective-permute-done.9.refs_9_ = bf16[512,128]{1,0:T(8,128)(2,1)S(1)} collective-permute-done((bf16[512,128]{1,0:T(8,128)(2,1)S(1)}, bf16[512,128]{1,0:T(8,128)(2,1)S(1)}, u32[]{:S(2)}, u32[]{:S(2)}) %collective-permute-start.9) | collective-permute-done | bytes 131104 | tf_op jit(solution)/shard_map/ppermute | solution.py:437
  94.4 0.0 collective-permute-done.5.refs_5_
  94.4 0.0 collective-permute-done.6.refs_6_
  94.4 0.5 collective-permute-done.8.refs_8_
  94.9 0.4 join_last.1
  95.3 34.7 %all_to_all.23 = bf16[64,8,2304]{2,1,0:T(8,128)(2,1)S(1)} all-to-all(bf16[64,8,2304]{2,1,0:T(8,128)(2,1)S(1)} %bitcast.15), channel_id=1, replica_groups=mesh['scene'=2,'row'=8,'col'=8] {'row','col'}, dimensions={0} | all-to-all | bytes 4718592 | tf_op jit(solution)/shard_map/all_to_all | solution.py:453
  130.0 2.0 %finish.1 = (bf16[768,768]{1,0:T(8,128)(2,1)}, f32[12,2304]{1,0:T(8,128)}, f32[12,768]{1,0:T(8,128)}) custom-call(s32[6]{0:T(128)S(1)} %stack.27.bits, bf16[512,2304]{1,0:T(8,128)(2,1)S(1)} %bitcast.14), custom_call_target="tpu_custom_call" | custom-call | flops 10000000 | bytes 2000000 | tf_op jit(solution)/shard_map/finish/pallas_call | solution.py:408
  (7 shorter events, 0.0 us)
Async XLA Ops:
  0.8 1.3 copy-start
  2.0 1.3 copy-start.1
  4.4 44.6 %copy-start.2 = (bf16[768,2304]{1,0:T(8,128)(2,1)S(1)}, bf16[768,2304]{1,0:T(8,128)(2,1)}, u32[]{:S(2)}) copy-start(bf16[768,2304]{1,0:T(8,128)(2,1)} %qkv_w.3) | copy-start | bytes 10616836
  4.4 44.6 %copy-start.3 = (bf16[768,768]{1,0:T(8,128)(2,1)S(1)}, bf16[768,768]{1,0:T(8,128)(2,1)}, u32[]{:S(2)}) copy-start(bf16[768,768]{1,0:T(8,128)(2,1)} %out_w.1) | copy-start | bytes 3538948
  67.7 12.4 %collective-permute-start = (bf16[512,512]{1,0:T(8,128)(2,1)S(1)}, bf16[512,512]{1,0:T(8,128)(2,1)S(1)}, u32[]{:S(2)}, u32[]{:S(2)}) collective-permute-start(bf16[512,512]{1,0:T(8,128)(2,1)S(1)} %get-tuple-element.55), channel_id=1, source_target_pairs={{0,16},{1,17},{2,18},{3,19},{4,20},{5,21},{6,22},{7,23},{8,24},{9,... | collective-permute-start | bytes 1572872 | tf_op jit(solution)/shard_map/ppermute | solution.py:437
  68.4 13.2 %collective-permute-start.1 = (bf16[512,512]{1,0:T(8,128)(2,1)S(1)}, bf16[512,512]{1,0:T(8,128)(2,1)S(1)}, u32[]{:S(2)}, u32[]{:S(2)}) collective-permute-start(bf16[512,512]{1,0:T(8,128)(2,1)S(1)} %get-tuple-element.56), channel_id=1, source_target_pairs={{0,48},{1,49},{2,50},{3,51},{4,52},{5,53},{6,54},{7,55},{8,56},{9,... | collective-permute-start | bytes 1572872 | tf_op jit(solution)/shard_map/ppermute | solution.py:437
  69.7 12.0 %collective-permute-start.2 = (bf16[512,512]{1,0:T(8,128)(2,1)S(1)}, bf16[512,512]{1,0:T(8,128)(2,1)S(1)}, u32[]{:S(2)}, u32[]{:S(2)}) collective-permute-start(bf16[512,512]{1,0:T(8,128)(2,1)S(1)} %get-tuple-element.57), channel_id=1, source_target_pairs={{0,8},{1,9},{2,10},{3,11},{4,12},{5,13},{6,14},{7,15},{8,0},{9,1},... | collective-permute-start | bytes 1572872 | tf_op jit(solution)/shard_map/ppermute | solution.py:437
  73.1 13.3 %collective-permute-start.3 = (bf16[512,512]{1,0:T(8,128)(2,1)S(1)}, bf16[512,512]{1,0:T(8,128)(2,1)S(1)}, u32[]{:S(2)}, u32[]{:S(2)}) collective-permute-start(bf16[512,512]{1,0:T(8,128)(2,1)S(1)} %get-tuple-element.52), channel_id=1, source_target_pairs={{0,2},{1,3},{2,0},{3,1},{4,6},{5,7},{6,4},{7,5},{8,10},{9,11},{10,... | collective-permute-start | bytes 1572872 | tf_op jit(solution)/shard_map/ppermute | solution.py:437
  73.7 11.3 %collective-permute-start.4 = (bf16[512,256]{1,0:T(8,128)(2,1)S(1)}, bf16[512,256]{1,0:T(8,128)(2,1)S(1)}, u32[]{:S(2)}, u32[]{:S(2)}) collective-permute-start(bf16[512,256]{1,0:T(8,128)(2,1)S(1)} %get-tuple-element.53), channel_id=1, source_target_pairs={{0,6},{1,7},{2,4},{3,5},{4,2},{5,3},{6,0},{7,1},{8,14},{9,15},{10,... | collective-permute-start | bytes 786440 | tf_op jit(solution)/shard_map/ppermute | solution.py:437
  83.0 11.4 %collective-permute-start.5 = (bf16[512,256]{1,0:T(8,128)(2,1)S(1)}, bf16[512,256]{1,0:T(8,128)(2,1)S(1)}, u32[]{:S(2)}, u32[]{:S(2)}) collective-permute-start(bf16[512,256]{1,0:T(8,128)(2,1)S(1)} %get-tuple-element.73), channel_id=1, source_target_pairs={{0,8},{1,9},{2,10},{3,11},{4,12},{5,13},{6,14},{7,15},{8,0},{9,1},... | collective-permute-start | bytes 786440 | tf_op jit(solution)/shard_map/ppermute | solution.py:437
  84.0 10.4 %collective-permute-start.6 = (bf16[512,256]{1,0:T(8,128)(2,1)S(1)}, bf16[512,256]{1,0:T(8,128)(2,1)S(1)}, u32[]{:S(2)}, u32[]{:S(2)}) collective-permute-start(bf16[512,256]{1,0:T(8,128)(2,1)S(1)} %get-tuple-element.74), channel_id=1, source_target_pairs={{0,2},{1,3},{2,0},{3,1},{4,6},{5,7},{6,4},{7,5},{8,10},{9,11},{10,... | collective-permute-start | bytes 786440 | tf_op jit(solution)/shard_map/ppermute | solution.py:437
  84.5 9.9 %collective-permute-start.7 = (bf16[512,256]{1,0:T(8,128)(2,1)S(1)}, bf16[512,256]{1,0:T(8,128)(2,1)S(1)}, u32[]{:S(2)}, u32[]{:S(2)}) collective-permute-start(bf16[512,256]{1,0:T(8,128)(2,1)S(1)} %get-tuple-element.75), channel_id=1, source_target_pairs={{0,16},{1,17},{2,18},{3,19},{4,20},{5,21},{6,22},{7,23},{8,24},{9,... | collective-permute-start | bytes 786440 | tf_op jit(solution)/shard_map/ppermute | solution.py:437
  87.3 7.7 %collective-permute-start.8 = (bf16[512,256]{1,0:T(8,128)(2,1)S(1)}, bf16[512,256]{1,0:T(8,128)(2,1)S(1)}, u32[]{:S(2)}, u32[]{:S(2)}) collective-permute-start(bf16[512,256]{1,0:T(8,128)(2,1)S(1)} %get-tuple-element.76), channel_id=1, source_target_pairs={{0,48},{1,49},{2,50},{3,51},{4,52},{5,53},{6,54},{7,55},{8,56},{9,... | collective-permute-start | bytes 786440 | tf_op jit(solution)/shard_map/ppermute | solution.py:437
  88.2 6.2 %collective-permute-start.9 = (bf16[512,128]{1,0:T(8,128)(2,1)S(1)}, bf16[512,128]{1,0:T(8,128)(2,1)S(1)}, u32[]{:S(2)}, u32[]{:S(2)}) collective-permute-start(bf16[512,128]{1,0:T(8,128)(2,1)S(1)} %get-tuple-element.77), channel_id=1, source_target_pairs={{0,9},{1,8},{2,11},{3,10},{4,13},{5,12},{6,15},{7,14},{8,1},{9,0},... | collective-permute-start | bytes 393224 | tf_op jit(solution)/shard_map/ppermute | solution.py:437

commit v6 on v5

--- a/solution.py
+++ b/solution.py
@@ -18,7 +18,7 @@
 LANES = 128
 LOG2_E = 1.4426950408889634
 FIRST = (((16, 4), (8, 3), 2), ((48, 5), (2, 1), 2), ((8, 3), (16, 4), 2))
-LAST = (((2, 1), (48, 5), 2), ((6, 2), (9, 0), 1))
+LAST = (((2, 1), (48, 5), 1), ((6, 2), (9, 0), 1), ((9, 0), (6, 2), 1))
 STREAMS = FIRST + LAST
 TILE = 256
 

time: 132 us -> 138 us (1.045)
  waiting for transfers between devices: 8.51 us -> 12.5 us
  starting transfers between devices: 7.54 us -> 9.45 us
    ppermute x10 -> x12, waiting for transfers between devices: 8.51 us -> 12.5 us  [swap(): lax.ppermute(x, ('row', 'col'), [(i, i ^ stream[level][0]) for i in range...]
    ppermute x10 -> x12, starting transfers between devices: 7.54 us -> 9.45 us  [swap(): lax.ppermute(x, ('row', 'col'), [(i, i ^ stream[level][0]) for i in range...]
  transfers between devices with their start and end apart: 10 -> 12, of which waited for: 4 -> 5; matrix products, arithmetic and copies ran while one was open for 0% -> 0% of each run, Pallas kernels for 8% -> 7%
where the time goes in v6:
time: 138 us
  blocking collectives  79.4 us (58%)
  Pallas kernels  33.2 us (24%)
  waiting for transfers between devices  12.5 us (9%)
  starting transfers between devices  9.45 us (7%)
  local copies, waits for them, and re-layouts  2.63 us (2%)
    all_to_all x1, blocking collectives, local(): exchange(sent)  44.5 us
    all_to_all x1, blocking collectives, local(): exchange(join_last(grads, (*early[:first], *late[:last], *early_came, *la...  34.8 us
    pallas_call x1, Pallas kernels, main_part(): pl.pallas_call(main_kernel, in_specs=[pl.BlockSpec(memory_space=pltpu.SME...  18.7 us
    ppermute x12, waiting for transfers between devices, swap(): lax.ppermute(x, ('row', 'col'), [(i, i ^ stream[level][0]) for i in range...  12.5 us
    ppermute x12, starting transfers between devices, swap(): lax.ppermute(x, ('row', 'col'), [(i, i ^ stream[level][0]) for i in range...  9.45 us
    pallas_call x1, Pallas kernels, token_part(): pl.pallas_call(token_kernel, in_specs=[vmem] * 5, out_specs=vmem, out_sha...  6.09 us
  transfers between devices with their start and end apart: 12, of which 5 were waited for; matrix products, arithmetic and copies ran while one was open for 0% of the time, Pallas kernels for 7%

profile of v6, /device:TPU:0, one launch (start us, length us, event | category | flops | bytes accessed | tf_op | source)
XLA Modules:
  0.0 138.1 jit_solution(2384117376807926831)
XLA Ops:
  0.8 0.0 copy-start
  0.8 1.3 copy-done
  2.0 1.3 copy-done.1
  3.3 1.0 pack_tokens.1
  4.3 0.1 stack.27.bits
  4.4 44.5 %all_to_all.22 = bf16[64,8,2304]{2,1,0:T(8,128)(2,1)S(1)} all-to-all(bf16[64,8,2304]{2,1,0:T(8,128)(2,1)S(1)} %bitcast.13), channel_id=1, replica_groups=mesh['scene'=2,'row'=8,'col'=8] {'row','col'}, dimensions={0} | all-to-all | bytes 4718592 | tf_op jit(solution)/shard_map/all_to_all | solution.py:433
  49.0 18.7 %main_part.1 = (bf16[768,768]{1,0:T(8,128)(2,1)S(1)}, bf16[768,768]{1,0:T(8,128)(2,1)S(1)}, f32[768,256]{1,0:T(8,128)S(1)}, bf16[768,2304]{1,0:T(8,128)(2,1)S(1)...) custom-call(s32[6]{0:T(128)S(1)} %stack.27.bits, ...), custom_call_target="tpu_custom_call" | custom-call | flops 16000000000 | bytes 30000000 | tf_op jit(solution)/shard_map/main_part/pallas_call | solution.py:225
  67.7 0.7 collective-permute-start
  68.4 1.2 collective-permute-start.1
  69.7 0.7 collective-permute-start.2
  70.3 2.7 %rest_part.1 = (bf16[512,256]{1,0:T(8,128)(2,1)S(1)}, bf16[512,256]{1,0:T(8,128)(2,1)S(1)}, bf16[512,256]{1,0:T(8,128)(2,1)S(1)}, bf16[512,256]{1,0:T(8,128)(2,1...) custom-call(s32[6]{0:T(128)S(1)} %stack.27.bits, bf16[768,768]{1,0:T(8,128)(2,1)S(1)} %get-tuple-element.50.cs, ...), custom_call_target="tpu_custom_call" | custom-call | flops 1000000 | bytes 100000 | tf_op jit(solution)/shard_map/rest_part/pallas_call | solution.py:269
  73.0 0.6 collective-permute-start.3
  73.6 0.3 collective-permute-start.4
  74.0 5.9 %collective-permute-done.refs_3_ = bf16[512,512]{1,0:T(8,128)(2,1)S(1)} collective-permute-done((bf16[512,512]{1,0:T(8,128)(2,1)S(1)}, bf16[512,512]{1,0:T(8,128)(2,1)S(1)}, u32[]{:S(2)}, u32[]{:S(2)}) %collective-permute-start) | collective-permute-done | bytes 524320 | tf_op jit(solution)/shard_map/ppermute | solution.py:437
  79.9 0.8 collective-permute-start.5
  80.6 6.1 %token_grad.1.grad = bf16[512,1152]{1,0:T(8,128)(2,1)S(1)} custom-call(bf16[768,768]{1,0:T(8,128)(2,1)S(1)} %get-tuple-element.49.xs, bf16[768,768]{1,0:T(8,128)(2,1)S(1)} %get-tuple-element.50.cs, f32[768,256]{1,0:T(8,128)S(1)} %get-tuple-element.51.stats, bf16[768,2304]{1,0:T(8,128)(2,1)S(1)} %get-tuple-element.61.dqkv, bf16[768,2304]{1,0:T(8,128)(2,1)S(1)} %copy-done.2), custom_call_target="tpu_custom_call" | custom-call | flops 1000000 | bytes 100000 | tf_op jit(solution)/shard_map/token_grad/pallas_call | solution.py:308
  86.7 0.0 collective-permute-done.3.refs_3_
  86.8 0.7 collective-permute-done.5.refs_5_
  87.5 1.0 join.3
  88.4 1.6 %collective-permute-start.9 = (bf16[512,128]{1,0:T(8,128)(2,1)S(1)}, bf16[512,128]{1,0:T(8,128)(2,1)S(1)}, u32[]{:S(2)}, u32[]{:S(2)}) collective-permute-start(bf16[512,128]{1,0:T(8,128)(2,1)S(1)} %get-tuple-element.85), channel_id=1, source_target_pairs={{0,48},{1,49},{2,50},{3,51},{4,52},{5,53},{6,54},{7,55},{8,56},{9,... | collective-permute-start | bytes 393224 | tf_op jit(solution)/shard_map/ppermute | solution.py:437
  90.0 1.4 %join.2 = (bf16[512,256]{1,0:T(8,128)(2,1)S(1)}, bf16[512,256]{1,0:T(8,128)(2,1)S(1)}, bf16[512,256]{1,0:T(8,128)(2,1)S(1)}, bf16[512,256]{1,0:T(8,128)(2,1)S(1)...) custom-call(s32[6]{0:T(128)S(1)} %stack.27.bits, bf16[512,512]{1,0:T(8,128)(2,1)S(1)} %get-tuple-element.67.refs_0_, ...), custom_call_target="tpu_custom_call" | custom-call | flops 10000 | bytes 10000 | tf_op jit(solution)/shard_map/join/pallas_call | solution.py:336
  91.4 0.1 collective-permute-start.6
  91.5 0.8 collective-permute-start.7
  92.3 0.1 collective-permute-start.8
  92.4 1.8 %collective-permute-start.10 = (bf16[512,128]{1,0:T(8,128)(2,1)S(1)}, bf16[512,128]{1,0:T(8,128)(2,1)S(1)}, u32[]{:S(2)}, u32[]{:S(2)}) collective-permute-start(bf16[512,128]{1,0:T(8,128)(2,1)S(1)} %get-tuple-element.86), channel_id=1, source_target_pairs={{0,9},{1,8},{2,11},{3,10},{4,13},{5,12},{6,15},{7,14},{8,1},{9,0},... | collective-permute-start | bytes 393224 | tf_op jit(solution)/shard_map/ppermute | solution.py:437
  94.2 0.5 collective-permute-done.9.refs_9_
  94.7 0.7 collective-permute-start.11
  95.4 3.2 %collective-permute-done.10.refs_10_ = bf16[512,128]{1,0:T(8,128)(2,1)S(1)} collective-permute-done((bf16[512,128]{1,0:T(8,128)(2,1)S(1)}, bf16[512,128]{1,0:T(8,128)(2,1)S(1)}, u32[]{:S(2)}, u32[]{:S(2)}) %collective-permute-start.10) | collective-permute-done | bytes 131104 | tf_op jit(solution)/shard_map/ppermute | solution.py:437
  98.6 2.3 %collective-permute-done.11.refs_11_ = bf16[512,128]{1,0:T(8,128)(2,1)S(1)} collective-permute-done((bf16[512,128]{1,0:T(8,128)(2,1)S(1)}, bf16[512,128]{1,0:T(8,128)(2,1)S(1)}, u32[]{:S(2)}, u32[]{:S(2)}) %collective-permute-start.11) | collective-permute-done | bytes 131104 | tf_op jit(solution)/shard_map/ppermute | solution.py:437
  100.9 0.4 join_last.1
  101.3 34.8 %all_to_all.23 = bf16[64,8,2304]{2,1,0:T(8,128)(2,1)S(1)} all-to-all(bf16[64,8,2304]{2,1,0:T(8,128)(2,1)S(1)} %bitcast.15), channel_id=1, replica_groups=mesh['scene'=2,'row'=8,'col'=8] {'row','col'}, dimensions={0} | all-to-all | bytes 4718592 | tf_op jit(solution)/shard_map/all_to_all | solution.py:453
  136.1 2.0 %finish.1 = (bf16[768,768]{1,0:T(8,128)(2,1)}, f32[12,2304]{1,0:T(8,128)}, f32[12,768]{1,0:T(8,128)}) custom-call(s32[6]{0:T(128)S(1)} %stack.27.bits, bf16[512,2304]{1,0:T(8,128)(2,1)S(1)} %bitcast.14), custom_call_target="tpu_custom_call" | custom-call | flops 10000000 | bytes 2000000 | tf_op jit(solution)/shard_map/finish/pallas_call | solution.py:408
  (11 shorter events, 0.0 us)
Async XLA Ops:
  0.8 1.3 copy-start
  2.0 1.3 copy-start.1
  4.4 44.6 %copy-start.2 = (bf16[768,2304]{1,0:T(8,128)(2,1)S(1)}, bf16[768,2304]{1,0:T(8,128)(2,1)}, u32[]{:S(2)}) copy-start(bf16[768,2304]{1,0:T(8,128)(2,1)} %qkv_w.3) | copy-start | bytes 10616836
  4.4 44.6 %copy-start.3 = (bf16[768,768]{1,0:T(8,128)(2,1)S(1)}, bf16[768,768]{1,0:T(8,128)(2,1)}, u32[]{:S(2)}) copy-start(bf16[768,768]{1,0:T(8,128)(2,1)} %out_w.1) | copy-start | bytes 3538948
  67.7 12.2 %collective-permute-start = (bf16[512,512]{1,0:T(8,128)(2,1)S(1)}, bf16[512,512]{1,0:T(8,128)(2,1)S(1)}, u32[]{:S(2)}, u32[]{:S(2)}) collective-permute-start(bf16[512,512]{1,0:T(8,128)(2,1)S(1)} %get-tuple-element.62), channel_id=1, source_target_pairs={{0,16},{1,17},{2,18},{3,19},{4,20},{5,21},{6,22},{7,23},{8,24},{9,... | collective-permute-start | bytes 1572872 | tf_op jit(solution)/shard_map/ppermute | solution.py:437
  68.4 18.3 %collective-permute-start.1 = (bf16[512,512]{1,0:T(8,128)(2,1)S(1)}, bf16[512,512]{1,0:T(8,128)(2,1)S(1)}, u32[]{:S(2)}, u32[]{:S(2)}) collective-permute-start(bf16[512,512]{1,0:T(8,128)(2,1)S(1)} %get-tuple-element.63), channel_id=1, source_target_pairs={{0,48},{1,49},{2,50},{3,51},{4,52},{5,53},{6,54},{7,55},{8,56},{9,... | collective-permute-start | bytes 1572872 | tf_op jit(solution)/shard_map/ppermute | solution.py:437
  69.7 17.1 %collective-permute-start.2 = (bf16[512,512]{1,0:T(8,128)(2,1)S(1)}, bf16[512,512]{1,0:T(8,128)(2,1)S(1)}, u32[]{:S(2)}, u32[]{:S(2)}) collective-permute-start(bf16[512,512]{1,0:T(8,128)(2,1)S(1)} %get-tuple-element.64), channel_id=1, source_target_pairs={{0,8},{1,9},{2,10},{3,11},{4,12},{5,13},{6,14},{7,15},{8,0},{9,1},... | collective-permute-start | bytes 1572872 | tf_op jit(solution)/shard_map/ppermute | solution.py:437
  73.0 13.7 %collective-permute-start.3 = (bf16[512,256]{1,0:T(8,128)(2,1)S(1)}, bf16[512,256]{1,0:T(8,128)(2,1)S(1)}, u32[]{:S(2)}, u32[]{:S(2)}) collective-permute-start(bf16[512,256]{1,0:T(8,128)(2,1)S(1)} %get-tuple-element.58), channel_id=1, source_target_pairs={{0,2},{1,3},{2,0},{3,1},{4,6},{5,7},{6,4},{7,5},{8,10},{9,11},{10,... | collective-permute-start | bytes 786440 | tf_op jit(solution)/shard_map/ppermute | solution.py:437
  73.6 13.1 %collective-permute-start.4 = (bf16[512,256]{1,0:T(8,128)(2,1)S(1)}, bf16[512,256]{1,0:T(8,128)(2,1)S(1)}, u32[]{:S(2)}, u32[]{:S(2)}) collective-permute-start(bf16[512,256]{1,0:T(8,128)(2,1)S(1)} %get-tuple-element.59), channel_id=1, source_target_pairs={{0,6},{1,7},{2,4},{3,5},{4,2},{5,3},{6,0},{7,1},{8,14},{9,15},{10,... | collective-permute-start | bytes 786440 | tf_op jit(solution)/shard_map/ppermute | solution.py:437
  79.9 7.6 %collective-permute-start.5 = (bf16[512,256]{1,0:T(8,128)(2,1)S(1)}, bf16[512,256]{1,0:T(8,128)(2,1)S(1)}, u32[]{:S(2)}, u32[]{:S(2)}) collective-permute-start(bf16[512,256]{1,0:T(8,128)(2,1)S(1)} %get-tuple-element.60), channel_id=1, source_target_pairs={{0,9},{1,8},{2,11},{3,10},{4,13},{5,12},{6,15},{7,14},{8,1},{9,0},... | collective-permute-start | bytes 786440 | tf_op jit(solution)/shard_map/ppermute | solution.py:437
  88.4 6.3 %collective-permute-start.9 = (bf16[512,128]{1,0:T(8,128)(2,1)S(1)}, bf16[512,128]{1,0:T(8,128)(2,1)S(1)}, u32[]{:S(2)}, u32[]{:S(2)}) collective-permute-start(bf16[512,128]{1,0:T(8,128)(2,1)S(1)} %get-tuple-element.85), channel_id=1, source_target_pairs={{0,48},{1,49},{2,50},{3,51},{4,52},{5,53},{6,54},{7,55},{8,56},{9,... | collective-permute-start | bytes 393224 | tf_op jit(solution)/shard_map/ppermute | solution.py:437
  91.4 9.4 %collective-permute-start.6 = (bf16[512,256]{1,0:T(8,128)(2,1)S(1)}, bf16[512,256]{1,0:T(8,128)(2,1)S(1)}, u32[]{:S(2)}, u32[]{:S(2)}) collective-permute-start(bf16[512,256]{1,0:T(8,128)(2,1)S(1)} %get-tuple-element.82), channel_id=1, source_target_pairs={{0,8},{1,9},{2,10},{3,11},{4,12},{5,13},{6,14},{7,15},{8,0},{9,1},... | collective-permute-start | bytes 786440 | tf_op jit(solution)/shard_map/ppermute | solution.py:437
  91.5 9.3 %collective-permute-start.7 = (bf16[512,256]{1,0:T(8,128)(2,1)S(1)}, bf16[512,256]{1,0:T(8,128)(2,1)S(1)}, u32[]{:S(2)}, u32[]{:S(2)}) collective-permute-start(bf16[512,256]{1,0:T(8,128)(2,1)S(1)} %get-tuple-element.83), channel_id=1, source_target_pairs={{0,2},{1,3},{2,0},{3,1},{4,6},{5,7},{6,4},{7,5},{8,10},{9,11},{10,... | collective-permute-start | bytes 786440 | tf_op jit(solution)/shard_map/ppermute | solution.py:437
  92.3 8.6 %collective-permute-start.8 = (bf16[512,256]{1,0:T(8,128)(2,1)S(1)}, bf16[512,256]{1,0:T(8,128)(2,1)S(1)}, u32[]{:S(2)}, u32[]{:S(2)}) collective-permute-start(bf16[512,256]{1,0:T(8,128)(2,1)S(1)} %get-tuple-element.84), channel_id=1, source_target_pairs={{0,16},{1,17},{2,18},{3,19},{4,20},{5,21},{6,22},{7,23},{8,24},{9,... | collective-permute-start | bytes 786440 | tf_op jit(solution)/shard_map/ppermute | solution.py:437
  92.4 6.2 %collective-permute-start.10 = (bf16[512,128]{1,0:T(8,128)(2,1)S(1)}, bf16[512,128]{1,0:T(8,128)(2,1)S(1)}, u32[]{:S(2)}, u32[]{:S(2)}) collective-permute-start(bf16[512,128]{1,0:T(8,128)(2,1)S(1)} %get-tuple-element.86), channel_id=1, source_target_pairs={{0,9},{1,8},{2,11},{3,10},{4,13},{5,12},{6,15},{7,14},{8,1},{9,0},... | collective-permute-start | bytes 393224 | tf_op jit(solution)/shard_map/ppermute | solution.py:437
  94.7 6.2 %collective-permute-start.11 = (bf16[512,128]{1,0:T(8,128)(2,1)S(1)}, bf16[512,128]{1,0:T(8,128)(2,1)S(1)}, u32[]{:S(2)}, u32[]{:S(2)}) collective-permute-start(bf16[512,128]{1,0:T(8,128)(2,1)S(1)} %get-tuple-element.87), channel_id=1, source_target_pairs={{0,6},{1,7},{2,4},{3,5},{4,2},{5,3},{6,0},{7,1},{8,14},{9,15},{10,... | collective-permute-start | bytes 393224 | tf_op jit(solution)/shard_map/ppermute | solution.py:437
